TPU v7x, 32 devices: a whole 2x2x4 slice. The times are simulated.
32 devices in a mesh: rows: 8 (over z, y), heads: 4 (over x, core).
Axes of the slice: x: 2, y: 2, z: 4, core: 2. Of those that a mesh axis runs over, the one named last changes fastest.
Arguments:
- imagery: bfloat16 [5, 512, 1024], P(None, 'rows'), may hold values from -120 to 120
- stem_weight: bfloat16 [11520, 1024], P('rows', 'heads'), may hold values from -0.0546875 to 0.0546875
- token_gain: bfloat16 [1024], replicated, may hold values from 0.099609375 to 1.8984375
- latents: bfloat16 [512, 1024], replicated, may hold values from -6 to 6
- latent_gain: bfloat16 [1024], replicated, may hold values from 0.099609375 to 1.8984375
- query_weight: bfloat16 [1024, 1024], P('rows', 'heads'), may hold values from -1.5 to 1.5
- key_weight: bfloat16 [1024, 1024], P('rows', 'heads'), may hold values from -1.5 to 1.5
- value_weight: bfloat16 [1024, 1024], P('rows', 'heads'), may hold values from -0.1875 to 0.1875
- out_weight: bfloat16 [1024, 1024], P('rows', 'heads'), may hold values from -0.1875 to 0.1875
Outputs:
- latent_out: bfloat16 [512, 1024], P('rows', 'heads')
All inputs are finite; a program needn't handle non-finite values.
Results may differ from a plain program's by a relative error of at most 0.035.
The roundings to bfloat16 on the way count: a program that leaves them out, or rounds other values in their place, can miss the bound.
Values may be sent and summed in bfloat16 or wider, within the bound.
A program may use at most 192 MiB of HBM per device.

v0:
```python
import jax
import jax.numpy as jnp
from jax import lax
from jax.sharding import PartitionSpec as P

D = 1024
HEADS = 16
LAT = 512
BANDS = 5
KER = 48
STRIDE = 32
TROWS = 2
TCOLS = 32


epsilon = 1e-05


def shifted(block, axis, distance):
    devices = range(lax.axis_size(axis))
    route = [(i - distance, i) for i in devices if i - distance in devices]
    return lax.ppermute(block, axis, route)


def layer_norm(inputs, gain_row):
    widened = inputs.astype(jnp.float32)
    average = jnp.mean(widened, axis=-1, keepdims=True)
    centered = widened - average
    variance = jnp.mean(centered * centered, axis=-1, keepdims=True)
    return (centered * lax.rsqrt(variance + epsilon) * gain_row.astype(jnp.float32)).astype(
        jnp.bfloat16
    )


def build_patches(strip_rows):
    rim_rows = KER - STRIDE
    padded = jnp.pad(strip_rows, ((0, 0), (0, STRIDE - rim_rows), (0, STRIDE)))
    blocks = padded.reshape(BANDS, TROWS + 1, STRIDE, TCOLS + 1, STRIDE)
    row_cat = jnp.concatenate([blocks[:, :TROWS], blocks[:, 1:, :rim_rows]], axis=2)
    col_cat = jnp.concatenate(
        [row_cat[:, :, :, :TCOLS, :], row_cat[:, :, :, 1:, :rim_rows]], axis=4
    )
    ordered = jnp.transpose(col_cat, (1, 3, 0, 2, 4))
    return ordered.reshape(TROWS * TCOLS, BANDS * KER * KER)


def per_device(
    imagery,
    stem_weight,
    token_gain,
    latents,
    latent_gain,
    query_weight,
    key_weight,
    value_weight,
    out_weight,
):
    rim_rows = KER - STRIDE
    below = shifted(imagery[:, :rim_rows, :], "rows", -1)
    patches = build_patches(jnp.concatenate([imagery, below], axis=1))
    token_count = patches.shape[0]
    width_dev = stem_weight.shape[1]
    stem_out = jnp.dot(
        patches,
        lax.all_gather(stem_weight, "rows", axis=0, tiled=True),
        preferred_element_type=jnp.float32,
    )
    feature = lax.all_gather(stem_out.astype(jnp.bfloat16), "heads", axis=1, tiled=True)
    token_norm = layer_norm(feature, token_gain)
    w_query, w_key, w_value, w_out = (
        lax.all_gather(query_weight, "rows", axis=0, tiled=True),
        lax.all_gather(key_weight, "rows", axis=0, tiled=True),
        lax.all_gather(value_weight, "rows", axis=0, tiled=True),
        lax.all_gather(out_weight, "rows", axis=0, tiled=True),
    )
    keys = jnp.dot(token_norm, w_key, preferred_element_type=jnp.float32).astype(jnp.bfloat16)
    values = jnp.dot(token_norm, w_value, preferred_element_type=jnp.float32).astype(jnp.bfloat16)
    head_size = D // HEADS
    heads_dev = width_dev // head_size
    latent_dev = LAT // lax.axis_size("rows")
    first_latent = lax.axis_index("rows") * latent_dev
    queries = jnp.dot(
        layer_norm(latents, latent_gain), w_query, preferred_element_type=jnp.float32
    ).astype(jnp.bfloat16)
    query_split = queries.reshape(LAT, heads_dev, head_size)
    key_split = keys.reshape(token_count, heads_dev, head_size)
    value_split = values.reshape(token_count, heads_dev, head_size)
    scores = jnp.einsum(
        "lhd,thd->lht", query_split, key_split, preferred_element_type=jnp.float32
    ) * head_size ** (-0.5)
    local_peak = jnp.max(scores, axis=2)

    def own_slice(array):
        return lax.dynamic_slice_in_dim(array, first_latent, latent_dev, 0)

    global_peak = lax.pmax(local_peak, "rows")
    weights = jnp.exp(scores - global_peak[:, :, None])
    totals = jnp.sum(weights, axis=2)
    upper_part = weights.astype(jnp.bfloat16)
    lower_part = (weights - upper_part.astype(jnp.float32)).astype(jnp.bfloat16)
    numerator = jnp.einsum(
        "lht,thd->lhd", upper_part, value_split, preferred_element_type=jnp.float32
    )
    numerator = numerator + jnp.einsum(
        "lht,thd->lhd", lower_part, value_split, preferred_element_type=jnp.float32
    )
    totals, numerator = (totals, numerator.reshape(LAT, width_dev))
    totals, numerator = lax.psum((totals, numerator), "rows")
    totals = own_slice(totals)
    numerator = own_slice(numerator)
    attended = numerator.reshape(latent_dev, heads_dev, head_size) / totals[:, :, None]
    mixed = attended.reshape(latent_dev, width_dev).astype(jnp.bfloat16)
    out_terms = lax.dot_general(
        mixed, w_out, (((1,), (1,)), ((), ())), preferred_element_type=jnp.float32
    )
    return lax.psum_scatter(out_terms, "heads", scatter_dimension=1, tiled=True).astype(
        jnp.bfloat16
    )


def solution(mesh):
    return jax.shard_map(
        per_device,
        mesh=mesh,
        in_specs=(
            P(None, "rows", None),
            P("rows", "heads"),
            P(),
            P(),
            P(),
            P("rows", "heads"),
            P("rows", "heads"),
            P("rows", "heads"),
            P("rows", "heads"),
        ),
        out_specs=P("rows", "heads"),
        check_vma=False,
    )
```

profile of v0, /device:TPU:0, one launch (start us, length us, event | category | flops | bytes accessed | tf_op | source)
XLA Modules:
  0.0 272.1 jit_solution(13734566096694369753)
XLA Ops:
  7.3 0.9 slice.15
  8.2 1.3 collective-permute-start
  10.9 1.4 convert_reduce_fusion
  12.8 37.1 %all_gather.21 = bf16[1024,256]{1,0:T(8,128)(2,1)S(1)} all-gather(bf16[128,256]{1,0:T(8,128)(2,1)S(1)} %copy-done.2), channel_id=1, replica_groups=mesh['rows'=8,'heads'=4] {'rows'}, dimensions={0}, use_global_device_ids=true | all-gather | bytes 589824 | tf_op jit(solution)/shard_map/all_gather | solution.py:72
  50.0 33.5 %all_gather.22 = bf16[1024,256]{1,0:T(8,128)(2,1)S(1)} all-gather(bf16[128,256]{1,0:T(8,128)(2,1)S(1)} %copy-done.3), channel_id=1, replica_groups=mesh['rows'=8,'heads'=4] {'rows'}, dimensions={0}, use_global_device_ids=true | all-gather | bytes 589824 | tf_op jit(solution)/shard_map/all_gather | solution.py:71
  84.1 32.8 %all_gather.20 = bf16[1024,256]{1,0:T(8,128)(2,1)S(1)} all-gather(bf16[128,256]{1,0:T(8,128)(2,1)S(1)} %copy-done.4), channel_id=1, replica_groups=mesh['rows'=8,'heads'=4] {'rows'}, dimensions={0}, use_global_device_ids=true | all-gather | bytes 589824 | tf_op jit(solution)/shard_map/all_gather | solution.py:73
  117.0 4.7 %reshape.49 = bf16[5,3,32,33,32]{4,3,2,1,0:T(8,128)(2,1)} reshape(bf16[5,96,1056]{2,1,0:T(8,128)(2,1)S(1)} %fusion.14) | data formatting | bytes 2027520 | tf_op jit(solution)/shard_map/reshape | solution.py:38
  121.6 2.5 slice.20
  124.1 1.7 slice.21
  125.9 0.8 fusion
  126.7 3.5 %fusion.2 = bf16[2,32,5,48,48]{4,1,3,0,2:T(8,128)(2,1)S(1)} fusion(bf16[5,2,16,33,32]{4,3,2,1,0:T(8,128)(2,1)S(1)} %slice.21, bf16[5,2,32,33,32]{4,3,2,1,0:T(8,128)(2,1)S(1)} %slice.20, bf16[5,2,48,32,32]{4,3,2,1,0:T(8,128)(2,1)S(1)} %fusion), kind=kLoop, calls=%fused_computation.5 | loop fusion | flops 4423680 | bytes 3471360 | tf_op jit(solution)/shard_map/transpose | solution.py:43
  130.2 3.5 %copy.13 = bf16[2,32,5,48,48]{4,3,2,1,0:T(8,128)(2,1)} copy(bf16[2,32,5,48,48]{4,1,3,0,2:T(8,128)(2,1)S(1)} %fusion.2) | data formatting | bytes 2949120 | tf_op jit(solution)/shard_map/transpose | solution.py:43
  133.7 5.4 %reshape.50 = bf16[64,11520]{1,0:T(8,128)(2,1)S(1)} reshape(bf16[2,32,5,48,48]{4,3,2,1,0:T(8,128)(2,1)} %copy.13) | data formatting | bytes 2949120 | tf_op jit(solution)/shard_map/reshape | solution.py:44
  139.1 3.8 %convolution_convert_fusion.3 = bf16[64,256]{1,0:T(8,128)(2,1)S(1)} fusion(bf16[64,11520]{1,0:T(8,128)(2,1)S(1)} %reshape.50, bf16[11520,256]{1,0:T(8,128)(2,1)} %all-gather.2.cloned.1.call-done), kind=kOutput, calls=%fused_computation.26 | convolution fusion | flops 377503744 | bytes 7405568 | tf_op jit(solution)/shard_map/dot_general | solution.py:63
  142.9 5.4 %all_gather.19 = bf16[64,1024]{1,0:T(8,128)(2,1)S(1)} all-gather(bf16[64,256]{1,0:T(8,128)(2,1)S(1)} %convolution_convert_fusion.3), channel_id=1, replica_groups=mesh['rows'=8,'heads'=4] {'heads'}, dimensions={1}, use_global_device_ids=true | all-gather | bytes 163840 | tf_op jit(solution)/shard_map/all_gather | solution.py:68
  149.3 20.5 %pmax.7 = f32[512,4]{0,1:T(4,128)S(1)} all-reduce(f32[512,4]{0,1:T(4,128)S(1)} %get-tuple-element.5), channel_id=1, replica_groups=mesh['rows'=8,'heads'=4] {'rows'}, use_global_device_ids=true, to_apply=%region_5.6 | all-reduce | flops 2048 | bytes 16384 | tf_op jit(solution)/shard_map/pmax | solution.py:96
  170.4 1.0 convolution_add_fusion
  171.6 31.8 %all_gather.23 = bf16[1024,256]{1,0:T(8,128)(2,1)S(1)} all-gather(bf16[128,256]{1,0:T(8,128)(2,1)S(1)} %copy-done.5), channel_id=1, replica_groups=mesh['rows'=8,'heads'=4] {'rows'}, dimensions={0}, use_global_device_ids=true | all-gather | bytes 589824 | tf_op jit(solution)/shard_map/all_gather | solution.py:74
  203.5 17.6 %psum.15 = f32[512,4]{0,1:T(4,128)S(1)} all-reduce(f32[512,4]{0,1:T(4,128)S(1)} %fusion.19), channel_id=1, replica_groups=mesh['rows'=8,'heads'=4] {'rows'}, use_global_device_ids=true, to_apply=%region_8.9 | all-reduce | flops 2048 | bytes 16384 | tf_op jit(solution)/shard_map/psum | solution.py:108
  221.2 21.0 %all-reduce.3.cloned.1.call-done = f32[512,256]{0,1:T(8,128)} async-done(((f32[512,256]{0,1:T(8,128)}), f32[512,256]{0,1:T(8,128)}) %all-reduce.3.cloned.1.call-update) | async-done | bytes 524304 | tf_op jit(solution)/shard_map/psum | solution.py:108
  242.2 1.0 fusion.30
  243.2 1.0 fusion.35
  244.2 19.9 %reduce-scatter.2.cloned.1.call-done = f32[64,256]{1,0:T(8,128)} async-done(((f32[64,1024]{1,0:T(8,128)}), f32[64,256]{1,0:T(8,128)}) %reduce-scatter.2.cloned.1.call-update) | async-done | bytes 65552 | tf_op jit(solution)/shard_map/reduce_scatter | solution.py:116
  264.1 1.5 convert_element_type.61
  (39 shorter events, 5.1 us)
Async XLA Ops:
  6.5 5.8 %copy-start = (bf16[512,1024]{1,0:T(8,128)(2,1)S(1)}, bf16[512,1024]{1,0:T(8,128)(2,1)}, u32[]{:S(2)}) copy-start(bf16[512,1024]{1,0:T(8,128)(2,1)} %param.12) | copy-start | bytes 3145732
  6.5 6.3 %copy-start.2 = (bf16[128,256]{1,0:T(8,128)(2,1)S(1)}, bf16[128,256]{1,0:T(8,128)(2,1)}, u32[]{:S(2)}) copy-start(bf16[128,256]{1,0:T(8,128)(2,1)} %param.15) | copy-start | bytes 196612
  6.5 43.4 %copy-start.3 = (bf16[128,256]{1,0:T(8,128)(2,1)S(1)}, bf16[128,256]{1,0:T(8,128)(2,1)}, u32[]{:S(2)}) copy-start(bf16[128,256]{1,0:T(8,128)(2,1)} %param.14) | copy-start | bytes 196612
  6.5 132.5 %all-gather.2.cloned.1.call-start = ((), (), s32[]{:S(2)}) async-start(), calls=%async_computation.1 | async-start | bytes 6635520 | tf_op jit(solution)/shard_map/all_gather | solution.py:65
  7.3 234.9 %all-reduce.3.cloned.1.call-start = ((), (), s32[]{:S(2)}) async-start(), calls=%async_computation.2 | async-start | bytes 1048576 | tf_op jit(solution)/shard_map/psum | solution.py:108
  8.2 108.6 %collective-permute-start = (bf16[5,16,1024]{2,1,0:T(8,128)(2,1)S(1)}, bf16[5,16,1024]{2,1,0:T(8,128)(2,1)S(1)}, u32[]{:S(2)}, u32[]{:S(2)}) collective-permute-start(bf16[5,16,1024]{2,1,0:T(8,128)(2,1)S(1)} %slice.15), channel_id=1, source_target_pairs={{4,0},{8,4},{12,8},{16,12},{20,16},{24,20},{28,24},{5,1},{9,5},{13... | collective-permute-start | bytes 491528 | tf_op jit(solution)/shard_map/ppermute | solution.py:22
  12.8 71.3 %copy-start.4 = (bf16[128,256]{1,0:T(8,128)(2,1)S(1)}, bf16[128,256]{1,0:T(8,128)(2,1)}, u32[]{:S(2)}) copy-start(bf16[128,256]{1,0:T(8,128)(2,1)} %param.16) | copy-start | bytes 196612
  50.0 66.9 %copy-start.1 = (bf16[5,64,1024]{2,1,0:T(8,128)(2,1)S(1)}, bf16[5,64,1024]{2,1,0:T(8,128)(2,1)}, u32[]{:S(2)}) copy-start(bf16[5,64,1024]{2,1,0:T(8,128)(2,1)} %param.9) | copy-start | bytes 1966084
  149.3 22.3 %copy-start.5 = (bf16[128,256]{1,0:T(8,128)(2,1)S(1)}, bf16[128,256]{1,0:T(8,128)(2,1)}, u32[]{:S(2)}) copy-start(bf16[128,256]{1,0:T(8,128)(2,1)} %param.17) | copy-start | bytes 196612
  171.5 92.7 %reduce-scatter.2.cloned.1.call-start = ((), (), s32[]{:S(2)}) async-start(), calls=%async_computation.3 | async-start | bytes 327680 | tf_op jit(solution)/shard_map/reduce_scatter | solution.py:116
Sparse Core Ops, SparseCore 0:
  9.5 115.5 all-gather.1
  171.6 70.5 all-reduce.2
  244.8 19.2 reduce-scatter.1
where the time goes:
time: 273 us; the launch traced here: 272 us
  blocking collectives  179 us (66%)
  waiting for transfers between devices  41.7 us (15%)
  local copies, waits for them, and re-layouts  19 us (7%)
  between operations  13.3 us (5%)
  other arithmetic  10.5 us (4%)
  matrix products  7.5 us (3%)
    all_gather x1, blocking collectives, per_device(): lax.all_gather(key_weight, 'rows', axis=0, tiled=True)  37.1 us
    all_gather x1, blocking collectives, per_device(): lax.all_gather(query_weight, 'rows', axis=0, tiled=True)  33.5 us
    all_gather x1, blocking collectives, per_device(): lax.all_gather(value_weight, 'rows', axis=0, tiled=True)  32.8 us
    all_gather x1, blocking collectives, per_device(): lax.all_gather(out_weight, 'rows', axis=0, tiled=True)  31.8 us
    psum x1, waiting for transfers between devices, per_device(): totals, numerator = lax.psum((totals, numerator), 'rows')  21 us
    pmax x1, blocking collectives, per_device(): global_peak = lax.pmax(local_peak, 'rows')  20.5 us
    reduce_scatter x1, waiting for transfers between devices, per_device(): lax.psum_scatter(out_terms, 'heads', scatter_dimension=1, tiled=True)  19.9 us
    psum x1, blocking collectives, per_device(): totals, numerator = lax.psum((totals, numerator), 'rows')  17.6 us
  transfers between devices with their start and end apart: 4, of which 2 were waited for; matrix products, arithmetic and copies ran while one was open for 10% of the time, Pallas kernels for 0%

commit v1 on v0

--- a/solution.py
+++ b/solution.py
@@ -1,6 +1,10 @@
+import functools
+
 import jax
 import jax.numpy as jnp
 from jax import lax
+from jax.experimental import pallas as pl
+from jax.experimental.pallas import tpu as pltpu
 from jax.sharding import PartitionSpec as P
 
 D = 1024
@@ -118,9 +122,427 @@
     )
 
 
+MESH = pl.DeviceIdType.MESH
+VARIANTS = 5
+F32 = jnp.float32
+BF16 = jnp.bfloat16
+
+
+def dot(a, b):
+    return jnp.dot(a, b, preferred_element_type=F32)
+
+
+def iota(shape, dim):
+    return lax.broadcasted_iota(jnp.int32, shape, dim)
+
+
+def band_and_line(flat):
+    band = jnp.zeros_like(flat)
+    for step in range(1, BANDS + 1):
+        band = band + (flat >= KER * step).astype(jnp.int32)
+    return band, flat - KER * band
+
+
+def strip_kernel(
+    rows,
+    heads,
+    image_ref,
+    stem_ref,
+    token_gain_ref,
+    latents_ref,
+    latent_gain_ref,
+    wq_ref,
+    wk_ref,
+    wv_ref,
+    wo_ref,
+    out_ref,
+    lines_out,
+    lines_in,
+    wide,
+    order,
+    ordered,
+    stem_sum,
+    part_out,
+    part_in,
+    feature,
+    w_first,
+    w_second,
+    kv,
+    out_terms,
+    out_in,
+    line_s,
+    line_r,
+    line_fs,
+    line_fr,
+    part_s,
+    part_r,
+    feat_s,
+    feat_r,
+    end_s,
+    end_r,
+    gz_s,
+    gz_r,
+    gy_s,
+    gy_r,
+):
+    r = lax.axis_index("rows")
+    h = lax.axis_index("heads")
+    core = lax.rem(h, 2)
+    core_peer = h + 1 - 2 * core
+    y_peer = r + 1 - 2 * lax.rem(r, 2)
+    per = stem_ref.shape[0] // KER
+    pad = lines_in.shape[2]
+    width = stem_ref.shape[1]
+    pixels = image_ref.shape[2]
+    groups = pixels // 128
+    started = []
+
+    barrier = pltpu.get_barrier_semaphore()
+    for d in range(1, rows):
+        pl.semaphore_signal(
+            barrier, inc=1, device_id=(lax.rem(r + d, rows), h), device_id_type=MESH
+        )
+    for d in range(1, heads):
+        pl.semaphore_signal(
+            barrier, inc=1, device_id=(r, lax.rem(h + d, heads)), device_id_type=MESH
+        )
+
+    slots = rows * 2 * pad
+    row = iota((slots, 1), 0)
+    receiver, second, line = row // (2 * pad), (row // pad) % 2, row % pad
+    band, at = band_and_line(per * receiver + line)
+    height = image_ref.shape[1]
+    source = band * height + jnp.where(second == 1, (at + STRIDE) % height, at)
+    pick = (iota((slots, BANDS * height), 1) == source).astype(BF16)
+    image = image_ref[...].reshape(BANDS * height, pixels)
+    lines_out[...] = dot(pick, image).astype(BF16).reshape(lines_out.shape)
+    w_first[r, 0] = wk_ref[...]
+    w_first[r, 1] = wv_ref[...]
+    w_second[r, 0] = wq_ref[...]
+    w_second[r, 1] = wo_ref[...]
+    pl.semaphore_wait(barrier, rows - 1 + heads - 1)
+
+    def remote(src, dst, send, recv, to):
+        copy = pltpu.make_async_remote_copy(
+            src_ref=src,
+            dst_ref=dst,
+            send_sem=send,
+            recv_sem=recv,
+            device_id=to,
+            device_id_type=MESH,
+        )
+        copy.start()
+        started.append(copy)
+        return copy
+
+    def gather_start(buf, which):
+        first = [
+            remote(
+                buf.at[r],
+                buf.at[r],
+                gz_s.at[which, d],
+                gz_r.at[which, d],
+                (lax.rem(r + 2 * d, rows), h),
+            )
+            for d in range(1, rows // 2)
+        ]
+        across = remote(
+            buf.at[r], buf.at[r], gy_s.at[which, 0], gy_r.at[which, 0], (y_peer, h)
+        )
+        return first, [across]
+
+    def gather_forward(buf, which, state):
+        first, across = state
+        for d, copy in enumerate(first, 1):
+            copy.wait_recv()
+            slot = lax.rem(r + rows - 2 * d, rows)
+            across.append(
+                remote(
+                    buf.at[slot],
+                    buf.at[slot],
+                    gy_s.at[which, d],
+                    gy_r.at[which, d],
+                    (y_peer, h),
+                )
+            )
+
+    def gather_wait(state):
+        for copy in state[1]:
+            copy.wait_recv()
+
+    line_copies = []
+    for d in range(1, rows):
+        to = lax.rem(r + d, rows)
+        line_copies.append(
+            remote(
+                lines_out.at[to, core],
+                lines_in.at[r, core],
+                line_s.at[d],
+                line_r.at[d],
+                (to, h),
+            )
+        )
+    first_state = gather_start(w_first, 0)
+    second_state = gather_start(w_second, 1)
+    lines_in[r] = lines_out[r]
+
+    wide[...] = jnp.zeros_like(wide)
+
+    def widen(f, carry):
+        block = stem_ref[pl.ds(pl.multiple_of(f * KER, 16), KER), :]
+        for v in range(VARIANTS - 2):
+            wide[
+                pl.ds(pl.multiple_of(f * 128 + STRIDE * v, 16), KER),
+                v * width : (v + 1) * width,
+            ] = block
+        v = VARIANTS - 2
+        wide[
+            pl.ds(pl.multiple_of(f * 128 + STRIDE * v, 16), STRIDE),
+            v * width : (v + 1) * width,
+        ] = block[:STRIDE]
+        v = VARIANTS - 1
+        wide[
+            pl.ds(pl.multiple_of(f * 128, 16), KER - STRIDE), v * width : (v + 1) * width
+        ] = block[STRIDE:]
+        return carry
+
+    lax.fori_loop(0, per, widen, 0)
+
+    token_rows = rows * TROWS
+    row = iota((per * token_rows, 1), 0)
+    line, token_row = row // token_rows, row % token_rows
+    _, at = band_and_line(per * r + line)
+    odd = token_row % 2
+    strip = token_row // 2 + jnp.where((odd == 1) & (at >= STRIDE), 1, 0)
+    target = (strip * 2 + odd) * pad + line
+    order[...] = (iota(order.shape, 1) == target).astype(BF16)
+
+    forwards = []
+    for d, copy in enumerate(line_copies, 1):
+        copy.wait_recv()
+        slot = lax.rem(r + rows - d, rows)
+        forwards.append(
+            remote(
+                lines_in.at[slot, core],
+                lines_in.at[slot, core],
+                line_fs.at[d],
+                line_fr.at[d],
+                (r, core_peer),
+            )
+        )
+    for copy in forwards:
+        copy.wait_recv()
+    ordered[...] = dot(order[...], lines_in[...].reshape(slots, pixels)).astype(BF16)
+
+    at_once = 6
+    stem_sum[...] = jnp.zeros_like(stem_sum)
+
+    def stem_step(step, carry):
+        blocks = []
+        for k in range(at_once):
+            f = step * at_once + k
+            x = ordered[pl.ds(pl.multiple_of(f * token_rows, 16), token_rows), :]
+            blocks.append(
+                jnp.concatenate([x[:, 128 * g : 128 * g + 128] for g in range(groups)], axis=0)
+            )
+        left = jnp.concatenate(blocks, axis=1)
+        depth = at_once * 128
+        stem_sum[...] += dot(left, wide[pl.ds(pl.multiple_of(step * depth, 128), depth), :])
+        return carry
+
+    lax.fori_loop(0, per // at_once, stem_step, 0)
+    last = VARIANTS - 2
+    rim = jnp.concatenate(
+        [
+            stem_sum[token_rows:, (last + 1) * width :],
+            jnp.zeros((token_rows, width), F32),
+        ],
+        axis=0,
+    )
+    sums = jnp.concatenate(
+        [
+            stem_sum[:, : last * width],
+            stem_sum[:, last * width : (last + 1) * width] + rim,
+        ],
+        axis=1,
+    ).astype(BF16)
+    each = groups * TROWS
+    row = iota((rows * each, 1), 0)
+    strip, group, inner = row // each, (row % each) // TROWS, row % TROWS
+    turn = iota((rows * each, rows * each), 1) == group * token_rows + strip * TROWS + inner
+    part_out[...] = dot(turn.astype(BF16), sums).astype(BF16).reshape(part_out.shape)
+
+    part_copies = []
+    for d in range(1, rows):
+        to = lax.rem(r + d, rows)
+        part_copies.append(
+            remote(part_out.at[to], part_in.at[r], part_s.at[d], part_r.at[d], (to, h))
+        )
+    part_in[r] = part_out[r]
+
+    def norm(x, gain_ref):
+        average = jnp.mean(x, axis=-1, keepdims=True)
+        centered = x - average
+        variance = jnp.mean(centered * centered, axis=-1, keepdims=True)
+        return (centered * lax.rsqrt(variance + epsilon) * gain_ref[...].astype(F32)).astype(BF16)
+
+    own = latents_ref.shape[0] // rows
+    latent_norm = norm(
+        latents_ref[pl.ds(pl.multiple_of(r * own, own), own), :].astype(F32), latent_gain_ref
+    )
+    gather_forward(w_first, 0, first_state)
+    for copy in part_copies:
+        copy.wait_recv()
+    total = jnp.sum(part_in[...].astype(F32), axis=0)
+    feature[h] = jnp.concatenate(
+        [total[:, v * width : (v + 1) * width] for v in range(last + 1)], axis=0
+    ).astype(BF16)
+
+    feat_copies = []
+    for d in range(1, heads):
+        feat_copies.append(
+            remote(
+                feature.at[h],
+                feature.at[h],
+                feat_s.at[d],
+                feat_r.at[d],
+                (r, lax.rem(h + d, heads)),
+            )
+        )
+    gather_wait(first_state)
+    for copy in feat_copies:
+        copy.wait_recv()
+    token_norm = norm(
+        jnp.concatenate([feature[k] for k in range(heads)], axis=1).astype(F32), token_gain_ref
+    )
+    for k in range(2):
+        kv[r, k] = dot(token_norm, w_first[:, k].reshape(D, width)).astype(BF16)
+    kv_state = gather_start(kv, 2)
+
+    gather_forward(w_second, 1, second_state)
+    gather_forward(kv, 2, kv_state)
+    gather_wait(second_state)
+    queries = dot(latent_norm, w_second[:, 0].reshape(D, width)).astype(BF16)
+    gather_wait(kv_state)
+
+    tokens = kv.shape[0] * kv.shape[2]
+    keys = kv[:, 0].reshape(tokens, width)
+    values = kv[:, 1].reshape(tokens, width)
+    size = D // HEADS
+    mixed = []
+    for pair in range(width // 128):
+        cols = slice(128 * pair, 128 * pair + 128)
+        q, k, v = queries[:, cols], keys[:, cols], values[:, cols]
+        side = iota((own, 128), 1) < size
+        halves = []
+        for low in (True, False):
+            keep = side if low else jnp.logical_not(side)
+            mine = jnp.where(keep, q.astype(F32), 0.0).astype(BF16)
+            scores = lax.dot_general(
+                mine, k, (((1,), (1,)), ((), ())), preferred_element_type=F32
+            ) * size ** (-0.5)
+            weights = jnp.exp(scores - jnp.max(scores, axis=1, keepdims=True))
+            totals = jnp.sum(weights, axis=1, keepdims=True)
+            upper = weights.astype(BF16)
+            lower = (weights - upper.astype(F32)).astype(BF16)
+            halves.append((dot(upper, v) + dot(lower, v)) / totals)
+        mixed.append(jnp.where(side, halves[0], halves[1]).astype(BF16))
+    mixed = jnp.concatenate(mixed, axis=1)
+
+    for k in range(heads):
+        per_head = w_second.shape[0] // heads
+        block = w_second[per_head * k : per_head * (k + 1), 1].reshape(width, width)
+        out_terms[k] = lax.dot_general(
+            mixed, block, (((1,), (1,)), ((), ())), preferred_element_type=F32
+        )
+    end_copies = []
+    for d in range(1, heads):
+        to = lax.rem(h + d, heads)
+        end_copies.append(
+            remote(out_terms.at[to], out_in.at[d - 1], end_s.at[d], end_r.at[d], (r, to))
+        )
+    result = out_terms[h]
+    for d, copy in enumerate(end_copies, 1):
+        copy.wait_recv()
+        result = result + out_in[d - 1]
+    out_ref[...] = result.astype(BF16)
+    for copy in started:
+        copy.wait_send()
+
+
+def fused(rows, heads):
+    def per_chip(imagery, stem, token_gain, latents, latent_gain, wq, wk, wv, wo):
+        per = stem.shape[0] // KER
+        pad = -(-per // 16) * 16
+        width = stem.shape[1]
+        pixels = imagery.shape[2]
+        groups = pixels // 128
+        own = latents.shape[0] // rows
+        tokens = TROWS * TCOLS
+        token_rows = rows * TROWS
+        dma = pltpu.SemaphoreType.DMA
+        return pl.pallas_call(
+            functools.partial(strip_kernel, rows, heads),
+            out_shape=jax.ShapeDtypeStruct((own, width), BF16),
+            in_specs=[pl.BlockSpec(memory_space=pltpu.VMEM)] * 9,
+            out_specs=pl.BlockSpec(memory_space=pltpu.VMEM),
+            scratch_shapes=[
+                pltpu.VMEM((rows, 2, pad, pixels), BF16),
+                pltpu.VMEM((rows, 2, pad, pixels), BF16),
+                pltpu.VMEM((per * 128, VARIANTS * width), BF16),
+                pltpu.VMEM((per * token_rows, rows * 2 * pad), BF16),
+                pltpu.VMEM((per * token_rows, pixels), BF16),
+                pltpu.VMEM((groups * token_rows, VARIANTS * width), F32),
+                pltpu.VMEM((rows, groups * TROWS, 4 * width), BF16),
+                pltpu.VMEM((rows, groups * TROWS, 4 * width), BF16),
+                pltpu.VMEM((heads, tokens, width), BF16),
+                pltpu.VMEM((rows, 2, wk.shape[0], width), BF16),
+                pltpu.VMEM((rows, 2, wk.shape[0], width), BF16),
+                pltpu.VMEM((rows, 2, tokens, width), BF16),
+                pltpu.VMEM((heads, own, width), F32),
+                pltpu.VMEM((heads - 1, own, width), F32),
+                dma((rows,)),
+                dma((rows,)),
+                dma((rows,)),
+                dma((rows,)),
+                dma((rows,)),
+                dma((rows,)),
+                dma((heads,)),
+                dma((heads,)),
+                dma((heads,)),
+                dma((heads,)),
+                dma((3, rows // 2)),
+                dma((3, rows // 2)),
+                dma((3, rows // 2)),
+                dma((3, rows // 2)),
+            ],
+            compiler_params=pltpu.CompilerParams(
+                collective_id=0, has_side_effects=True, vmem_limit_bytes=48 * 2**20
+            ),
+        )(
+            imagery,
+            stem,
+            token_gain.reshape(1, -1),
+            latents,
+            latent_gain.reshape(1, -1),
+            wq,
+            wk,
+            wv,
+            wo,
+        )
+
+    return per_chip
+
+
+def lines_fit(mesh):
+    rows = mesh.shape["rows"]
+    return BANDS * KER % rows == 0 and rows <= 8
+
+
 def solution(mesh):
+    body = fused(mesh.shape["rows"], mesh.shape["heads"]) if lines_fit(mesh) else per_device
     return jax.shard_map(
-        per_device,
+        body,
         mesh=mesh,
         in_specs=(
             P(None, "rows", None),

time: 273 us -> 80.5 us (0.29)
  blocking collectives: 179 us -> 0 us
  Pallas kernels: 0 us -> 71.9 us
  waiting for transfers between devices: 41.7 us -> 0 us
  between operations: 13.3 us -> 0.03 us
  local copies, waits for them, and re-layouts: 19 us -> 8.1 us
  other arithmetic: 10.5 us -> 0 us
  matrix products: 7.5 us -> 0 us
    all_gather x5 -> x0, blocking collectives: 141 us -> none  [the longest x1 37.1 us: per_device(): lax.all_gather(key_weight, 'rows', axis=0, tiled=True)]
    pallas_call x0 -> x1, Pallas kernels: none -> 71.9 us  [per_chip(): pl.pallas_call(functools.partial(strip_kernel, rows, heads), out_shape=ja...]
    psum x1 -> x0, waiting for transfers between devices: 21 us -> none  [per_device(): totals, numerator = lax.psum((totals, numerator), 'rows')]
    pmax x1 -> x0, blocking collectives: 20.5 us -> none  [per_device(): global_peak = lax.pmax(local_peak, 'rows')]
    reduce_scatter x1 -> x0, waiting for transfers between devices: 19.9 us -> none  [per_device(): lax.psum_scatter(out_terms, 'heads', scatter_dimension=1, tiled=True)]
    psum x1 -> x0, blocking collectives: 17.6 us -> none  [per_device(): totals, numerator = lax.psum((totals, numerator), 'rows')]
    reshape x4 -> x2, local copies, waits for them, and re-layouts: 10.3 us -> 0.7 us  [the longest x1 0.7 us: per_chip(): token_gain.reshape(1, -1)]
    dot_general x8 -> x0, matrix products: 7.5 us -> none  [the longest x1 3.82 us: per_device(): jnp.dot(patches, lax.all_gather(stem_weight, 'rows', axis=0, tiled=True),...]
  transfers between devices with their start and end apart: 4 -> 0, of which waited for: 2 -> 0; matrix products, arithmetic and copies ran while one was open for 10% -> 0% of each run, Pallas kernels for 0% -> 0%
where the time goes in v1:
time: 80.5 us; the launch traced here: 80 us
  Pallas kernels  71.9 us (89%)
  local copies, waits for them, and re-layouts  8.1 us (10%)
    pallas_call x1, Pallas kernels, per_chip(): pl.pallas_call(functools.partial(strip_kernel, rows, heads), out_shape=ja...  71.9 us
    unnamed x17, local copies, waits for them, and re-layouts  7.4 us

profile of v1, /device:TPU:0, one launch (start us, length us, event | category | flops | bytes accessed | tf_op | source)
XLA Modules:
  0.0 80.0 jit_solution(7099296369012951485)
XLA Ops:
  0.0 0.0 copy-start.7
  0.0 0.7 reshape.6.token_gain_ref
  0.7 0.0 copy-done.7
  0.7 0.0 copy-start
  0.7 1.2 %copy-done = bf16[512,1024]{1,0:T(8,128)(2,1)S(1)} copy-done((bf16[512,1024]{1,0:T(8,128)(2,1)S(1)}, bf16[512,1024]{1,0:T(8,128)(2,1)}, u32[]{:S(2)}) %copy-start) | copy-done | bytes 1048600
  1.9 0.0 copy-start.1
  1.9 1.1 %copy-done.1 = bf16[1440,256]{1,0:T(8,128)(2,1)S(1)} copy-done((bf16[1440,256]{1,0:T(8,128)(2,1)S(1)}, bf16[1440,256]{1,0:T(8,128)(2,1)}, u32[]{:S(2)}) %copy-start.1) | copy-done | bytes 737304
  3.1 0.0 copy-start.2
  3.1 1.1 %copy-done.2 = bf16[5,64,1024]{2,1,0:T(8,128)(2,1)S(1)} copy-done((bf16[5,64,1024]{2,1,0:T(8,128)(2,1)S(1)}, bf16[5,64,1024]{2,1,0:T(8,128)(2,1)}, u32[]{:S(2)}) %copy-start.2) | copy-done | bytes 655384
  4.1 0.0 copy-start.3
  4.1 0.8 %copy-done.3 = bf16[128,256]{1,0:T(8,128)(2,1)S(1)} copy-done((bf16[128,256]{1,0:T(8,128)(2,1)S(1)}, bf16[128,256]{1,0:T(8,128)(2,1)}, u32[]{:S(2)}) %copy-start.3) | copy-done | bytes 65560
  5.0 0.0 copy-start.4
  5.0 0.8 %copy-done.4 = bf16[128,256]{1,0:T(8,128)(2,1)S(1)} copy-done((bf16[128,256]{1,0:T(8,128)(2,1)S(1)}, bf16[128,256]{1,0:T(8,128)(2,1)}, u32[]{:S(2)}) %copy-start.4) | copy-done | bytes 65560
  5.8 0.0 copy-start.5
  5.8 0.8 %copy-done.5 = bf16[128,256]{1,0:T(8,128)(2,1)S(1)} copy-done((bf16[128,256]{1,0:T(8,128)(2,1)S(1)}, bf16[128,256]{1,0:T(8,128)(2,1)}, u32[]{:S(2)}) %copy-start.5) | copy-done | bytes 65560
  6.7 0.0 copy-start.6
  6.7 0.8 %copy-done.6 = bf16[128,256]{1,0:T(8,128)(2,1)S(1)} copy-done((bf16[128,256]{1,0:T(8,128)(2,1)S(1)}, bf16[128,256]{1,0:T(8,128)(2,1)}, u32[]{:S(2)}) %copy-start.6) | copy-done | bytes 65560
  7.5 71.9 %shard_map.91 = bf16[64,256]{1,0:T(8,128)(2,1)S(1)} custom-call(bf16[5,64,1024]{2,1,0:T(8,128)(2,1)S(1)} %copy-done.2, bf16[1440,256]{1,0:T(8,128)(2,1)S(1)} %copy-done.1, bf16[1,1024]{1,0:T(2,128)(2,1)S(1)} %reshape.6.token_gain_ref, bf16[512,1024]{1,0:T(8,128)(2,1)S(1)} %copy-done, bf16[1,1024]{1,0:T(2,128)(2,1)S(1)} %reshape.7.latent_gain_ref, ...), custom_call_target="tpu_custom_call" | custom-call | tf_op jit(solution)/shard_map/pallas_call | solution.py:484
  79.4 0.6 copy.11
  (1 shorter events, 0.0 us)
Async XLA Ops:
  0.0 0.7 copy-start.7
  0.7 1.2 %copy-start = (bf16[512,1024]{1,0:T(8,128)(2,1)S(1)}, bf16[512,1024]{1,0:T(8,128)(2,1)}, u32[]{:S(2)}) copy-start(bf16[512,1024]{1,0:T(8,128)(2,1)} %latents_ref.1) | copy-start | bytes 3145732
  1.9 1.1 %copy-start.1 = (bf16[1440,256]{1,0:T(8,128)(2,1)S(1)}, bf16[1440,256]{1,0:T(8,128)(2,1)}, u32[]{:S(2)}) copy-start(bf16[1440,256]{1,0:T(8,128)(2,1)} %stem_ref.1) | copy-start | bytes 2211844
  3.1 1.1 %copy-start.2 = (bf16[5,64,1024]{2,1,0:T(8,128)(2,1)S(1)}, bf16[5,64,1024]{2,1,0:T(8,128)(2,1)}, u32[]{:S(2)}) copy-start(bf16[5,64,1024]{2,1,0:T(8,128)(2,1)} %image_ref.1) | copy-start | bytes 1966084
  4.1 0.8 %copy-start.3 = (bf16[128,256]{1,0:T(8,128)(2,1)S(1)}, bf16[128,256]{1,0:T(8,128)(2,1)}, u32[]{:S(2)}) copy-start(bf16[128,256]{1,0:T(8,128)(2,1)} %wq_ref.1) | copy-start | bytes 196612
  5.0 0.8 %copy-start.4 = (bf16[128,256]{1,0:T(8,128)(2,1)S(1)}, bf16[128,256]{1,0:T(8,128)(2,1)}, u32[]{:S(2)}) copy-start(bf16[128,256]{1,0:T(8,128)(2,1)} %wk_ref.1) | copy-start | bytes 196612
  5.8 0.8 %copy-start.5 = (bf16[128,256]{1,0:T(8,128)(2,1)S(1)}, bf16[128,256]{1,0:T(8,128)(2,1)}, u32[]{:S(2)}) copy-start(bf16[128,256]{1,0:T(8,128)(2,1)} %wv_ref.1) | copy-start | bytes 196612
  6.7 0.8 %copy-start.6 = (bf16[128,256]{1,0:T(8,128)(2,1)S(1)}, bf16[128,256]{1,0:T(8,128)(2,1)}, u32[]{:S(2)}) copy-start(bf16[128,256]{1,0:T(8,128)(2,1)} %wo_ref.1) | copy-start | bytes 196612

commit v2 on v1

--- a/solution.py
+++ b/solution.py
@@ -156,6 +156,12 @@
     wv_ref,
     wo_ref,
     out_ref,
+    image,
+    stem,
+    latent_rows,
+    latent_norm,
+    query_part,
+    query_in,
     lines_out,
     lines_in,
     wide,
@@ -170,16 +176,19 @@
     kv,
     out_terms,
     out_in,
+    local,
     line_s,
     line_r,
-    line_fs,
-    line_fr,
+    query_s,
+    query_r,
     part_s,
     part_r,
     feat_s,
     feat_r,
     end_s,
     end_r,
+    z_s,
+    z_r,
     gz_s,
     gz_r,
     gy_s,
@@ -189,13 +198,41 @@
     h = lax.axis_index("heads")
     core = lax.rem(h, 2)
     core_peer = h + 1 - 2 * core
-    y_peer = r + 1 - 2 * lax.rem(r, 2)
+    half = h // 2
+    x_peer = lax.rem(h + 2, heads)
+    y = lax.rem(r, 2)
+    z = r // 2
+    y_peer = r + 1 - 2 * y
+    z_opposite = lax.rem(r + 4, rows)
+    z_pair = r + 2 - 4 * lax.rem(z, 2)
+    z_last = lax.rem(z_pair + 4, rows)
+    own = latents_ref.shape[0] // rows
     per = stem_ref.shape[0] // KER
     pad = lines_in.shape[2]
     width = stem_ref.shape[1]
     pixels = image_ref.shape[2]
     groups = pixels // 128
     started = []
+
+    loads = [
+        pltpu.make_async_copy(source, target, local.at[k])
+        for k, (source, target) in enumerate(
+            [
+                (image_ref, image),
+                (wk_ref, w_first.at[r, 0]),
+                (wv_ref, w_first.at[r, 1]),
+                (stem_ref, stem),
+                (wq_ref, w_second.at[r, 0]),
+                (wo_ref, w_second.at[r, 1]),
+                (
+                    latents_ref.at[pl.ds(pl.multiple_of(z * 2 * own, 2 * own), 2 * own)],
+                    latent_rows,
+                ),
+            ]
+        )
+    ]
+    for copy in loads:
+        copy.start()
 
     barrier = pltpu.get_barrier_semaphore()
     for d in range(1, rows):
@@ -214,12 +251,9 @@
     height = image_ref.shape[1]
     source = band * height + jnp.where(second == 1, (at + STRIDE) % height, at)
     pick = (iota((slots, BANDS * height), 1) == source).astype(BF16)
-    image = image_ref[...].reshape(BANDS * height, pixels)
-    lines_out[...] = dot(pick, image).astype(BF16).reshape(lines_out.shape)
-    w_first[r, 0] = wk_ref[...]
-    w_first[r, 1] = wv_ref[...]
-    w_second[r, 0] = wq_ref[...]
-    w_second[r, 1] = wo_ref[...]
+    loads[0].wait()
+    flat = image[...].reshape(BANDS * height, pixels)
+    lines_out[...] = dot(pick, flat).astype(BF16).reshape(lines_out.shape)
     pl.semaphore_wait(barrier, rows - 1 + heads - 1)
 
     def remote(src, dst, send, recv, to):
@@ -240,8 +274,8 @@
             remote(
                 buf.at[r],
                 buf.at[r],
-                gz_s.at[which, d],
-                gz_r.at[which, d],
+                gz_s.at[d],
+                gz_r.at[d],
                 (lax.rem(r + 2 * d, rows), h),
             )
             for d in range(1, rows // 2)
@@ -270,26 +304,62 @@
         for copy in state[1]:
             copy.wait_recv()
 
+    def z_start(buf, which, part):
+        return [
+            remote(buf.at[r], buf.at[r], z_s.at[which, 0], z_r.at[which, 0], (z_opposite, h)),
+            remote(buf.at[r], buf.at[r], z_s.at[which, 1], z_r.at[which, 1], (z_pair, h)),
+        ], [y_send(part(buf, r), which, 0)]
+
+    def y_send(ref, which, k):
+        return remote(ref, ref, gy_s.at[which, k], gy_r.at[which, k], (y_peer, h))
+
+    def z_pass(buf, which, part, state):
+        first, across = state
+        first[0].wait_recv()
+        ref = buf.at[z_opposite]
+        first.append(remote(ref, ref, z_s.at[which, 2], z_r.at[which, 2], (z_pair, h)))
+        across.append(y_send(part(buf, z_opposite), which, 1))
+        first[1].wait_recv()
+        across.append(y_send(part(buf, z_pair), which, 2))
+
+    def z_end(buf, which, part, state):
+        first, across = state
+        first[2].wait_recv()
+        across.append(y_send(part(buf, z_last), which, 3))
+
+    def whole_slot(buf, slot):
+        return buf.at[slot]
+
+    def second_only(buf, slot):
+        return buf.at[slot, 1]
+
+    quarter = pad // 2
+
+    def lines_at(ref, slot, part):
+        return ref.at[slot, core, pl.ds(pl.multiple_of(part * quarter, quarter), quarter)]
+
     line_copies = []
     for d in range(1, rows):
         to = lax.rem(r + d, rows)
         line_copies.append(
             remote(
-                lines_out.at[to, core],
-                lines_in.at[r, core],
-                line_s.at[d],
-                line_r.at[d],
+                lines_at(lines_out, to, half),
+                lines_at(lines_in, r, half),
+                line_s.at[0, d],
+                line_r.at[0, d],
                 (to, h),
             )
         )
-    first_state = gather_start(w_first, 0)
-    second_state = gather_start(w_second, 1)
     lines_in[r] = lines_out[r]
+    loads[1].wait()
+    loads[2].wait()
 
     wide[...] = jnp.zeros_like(wide)
+    first_state = z_start(w_first, 0, whole_slot)
+    loads[3].wait()
 
     def widen(f, carry):
-        block = stem_ref[pl.ds(pl.multiple_of(f * KER, 16), KER), :]
+        block = stem[pl.ds(pl.multiple_of(f * KER, 16), KER), :]
         for v in range(VARIANTS - 2):
             wide[
                 pl.ds(pl.multiple_of(f * 128 + STRIDE * v, 16), KER),
@@ -317,22 +387,28 @@
     target = (strip * 2 + odd) * pad + line
     order[...] = (iota(order.shape, 1) == target).astype(BF16)
 
-    forwards = []
+    def pass_line(slot, part, k, d, to):
+        ref = lines_at(lines_in, slot, part)
+        return remote(ref, ref, line_s.at[k, d], line_r.at[k, d], (r, to))
+
+    over_x, over_core = [], []
     for d, copy in enumerate(line_copies, 1):
         copy.wait_recv()
         slot = lax.rem(r + rows - d, rows)
-        forwards.append(
-            remote(
-                lines_in.at[slot, core],
-                lines_in.at[slot, core],
-                line_fs.at[d],
-                line_fr.at[d],
-                (r, core_peer),
-            )
-        )
-    for copy in forwards:
+        over_x.append(pass_line(slot, half, 1, d, x_peer))
+        over_core.append(pass_line(slot, half, 2, d, core_peer))
+    for d, copy in enumerate(over_x, 1):
+        copy.wait_recv()
+        slot = lax.rem(r + rows - d, rows)
+        over_core.append(pass_line(slot, 1 - half, 3, d, core_peer))
+    loads[4].wait()
+    loads[5].wait()
+    second_state = z_start(w_second, 1, second_only)
+    for copy in over_core:
         copy.wait_recv()
     ordered[...] = dot(order[...], lines_in[...].reshape(slots, pixels)).astype(BF16)
+
+    z_pass(w_first, 0, whole_slot, first_state)
 
     at_once = 6
     stem_sum[...] = jnp.zeros_like(stem_sum)
@@ -386,11 +462,9 @@
         variance = jnp.mean(centered * centered, axis=-1, keepdims=True)
         return (centered * lax.rsqrt(variance + epsilon) * gain_ref[...].astype(F32)).astype(BF16)
 
-    own = latents_ref.shape[0] // rows
-    latent_norm = norm(
-        latents_ref[pl.ds(pl.multiple_of(r * own, own), own), :].astype(F32), latent_gain_ref
-    )
-    gather_forward(w_first, 0, first_state)
+    z_end(w_first, 0, whole_slot, first_state)
+    loads[6].wait()
+    latent_norm[...] = norm(latent_rows[...].astype(F32), latent_gain_ref)
     for copy in part_copies:
         copy.wait_recv()
     total = jnp.sum(part_in[...].astype(F32), axis=0)
@@ -409,6 +483,7 @@
                 (r, lax.rem(h + d, heads)),
             )
         )
+    z_pass(w_second, 1, second_only, second_state)
     gather_wait(first_state)
     for copy in feat_copies:
         copy.wait_recv()
@@ -419,10 +494,19 @@
         kv[r, k] = dot(token_norm, w_first[:, k].reshape(D, width)).astype(BF16)
     kv_state = gather_start(kv, 2)
 
-    gather_forward(w_second, 1, second_state)
+    z_end(w_second, 1, second_only, second_state)
+    depth = wq_ref.shape[0]
+    part = jnp.zeros((2 * own, width), F32)
+    for k in range(rows // 2):
+        at = 2 * k + y
+        part = part + dot(
+            latent_norm[:, pl.ds(pl.multiple_of(at * depth, depth), depth)], w_second[at, 0]
+        )
+    query_part[...] = part.reshape(query_part.shape)
+    query_copy = remote(query_part.at[1 - y], query_in, query_s, query_r, (y_peer, h))
     gather_forward(kv, 2, kv_state)
-    gather_wait(second_state)
-    queries = dot(latent_norm, w_second[:, 0].reshape(D, width)).astype(BF16)
+    query_copy.wait_recv()
+    queries = (query_part[y] + query_in[...]).astype(BF16)
     gather_wait(kv_state)
 
     tokens = kv.shape[0] * kv.shape[2]
@@ -449,6 +533,7 @@
         mixed.append(jnp.where(side, halves[0], halves[1]).astype(BF16))
     mixed = jnp.concatenate(mixed, axis=1)
 
+    gather_wait(second_state)
     for k in range(heads):
         per_head = w_second.shape[0] // heads
         block = w_second[per_head * k : per_head * (k + 1), 1].reshape(width, width)
@@ -484,9 +569,18 @@
         return pl.pallas_call(
             functools.partial(strip_kernel, rows, heads),
             out_shape=jax.ShapeDtypeStruct((own, width), BF16),
-            in_specs=[pl.BlockSpec(memory_space=pltpu.VMEM)] * 9,
+            in_specs=[
+                pl.BlockSpec(memory_space=pltpu.VMEM if k in (2, 4) else pltpu.HBM)
+                for k in range(9)
+            ],
             out_specs=pl.BlockSpec(memory_space=pltpu.VMEM),
             scratch_shapes=[
+                pltpu.VMEM(imagery.shape, BF16),
+                pltpu.VMEM(stem.shape, BF16),
+                pltpu.VMEM((2 * own, D), BF16),
+                pltpu.VMEM((2 * own, D), BF16),
+                pltpu.VMEM((2, own, width), F32),
+                pltpu.VMEM((own, width), F32),
                 pltpu.VMEM((rows, 2, pad, pixels), BF16),
                 pltpu.VMEM((rows, 2, pad, pixels), BF16),
                 pltpu.VMEM((per * 128, VARIANTS * width), BF16),
@@ -501,18 +595,21 @@
                 pltpu.VMEM((rows, 2, tokens, width), BF16),
                 pltpu.VMEM((heads, own, width), F32),
                 pltpu.VMEM((heads - 1, own, width), F32),
-                dma((rows,)),
-                dma((rows,)),
-                dma((rows,)),
-                dma((rows,)),
+                dma((7,)),
+                dma((4, rows)),
+                dma((4, rows)),
+                dma,
+                dma,
                 dma((rows,)),
                 dma((rows,)),
                 dma((heads,)),
                 dma((heads,)),
                 dma((heads,)),
                 dma((heads,)),
-                dma((3, rows // 2)),
-                dma((3, rows // 2)),
+                dma((2, 3)),
+                dma((2, 3)),
+                dma((rows // 2,)),
+                dma((rows // 2,)),
                 dma((3, rows // 2)),
                 dma((3, rows // 2)),
             ],
@@ -535,8 +632,7 @@
 
 
 def lines_fit(mesh):
-    rows = mesh.shape["rows"]
-    return BANDS * KER % rows == 0 and rows <= 8
+    return mesh.shape["rows"] == 8 and mesh.shape["heads"] == 4
 
 
 def solution(mesh):

time: 80.5 us -> 64.8 us (0.80)
  Pallas kernels: 71.9 us -> 56.2 us
    pallas_call x1, Pallas kernels: 71.9 us -> 56.2 us  [per_chip(): pl.pallas_call(functools.partial(strip_kernel, rows, heads), out_shape=ja...]
where the time goes in v2:
time: 64.8 us; the launch traced here: 64.4 us
  Pallas kernels  56.2 us (87%)
  local copies, waits for them, and re-layouts  8.1 us (12%)
    pallas_call x1, Pallas kernels, per_chip(): pl.pallas_call(functools.partial(strip_kernel, rows, heads), out_shape=ja...  56.2 us
    unnamed x17, local copies, waits for them, and re-layouts  7.4 us

profile of v2, /device:TPU:0, one launch (start us, length us, event | category | flops | bytes accessed | tf_op | source)
XLA Modules:
  0.0 64.4 jit_solution(9969929495565890478)
XLA Ops:
  0.0 0.0 copy-start.7
  0.0 0.7 %reshape.6.token_gain_ref = bf16[1,1024]{1,0:T(2,128)(2,1)S(1)} reshape(bf16[1024]{0:T(1024)(128)(2,1)} %param.11) | data formatting | bytes 4096 | tf_op jit(solution)/shard_map/reshape | solution.py:622
  0.7 0.0 copy-done.7
  0.7 0.0 copy-start
  0.7 1.2 %copy-done = bf16[512,1024]{1,0:T(8,128)(2,1)S(1)} copy-done((bf16[512,1024]{1,0:T(8,128)(2,1)S(1)}, bf16[512,1024]{1,0:T(8,128)(2,1)}, u32[]{:S(2)}) %copy-start) | copy-done | bytes 1048600
  1.9 0.0 copy-start.1
  1.9 1.1 %copy-done.1 = bf16[1440,256]{1,0:T(8,128)(2,1)S(1)} copy-done((bf16[1440,256]{1,0:T(8,128)(2,1)S(1)}, bf16[1440,256]{1,0:T(8,128)(2,1)}, u32[]{:S(2)}) %copy-start.1) | copy-done | bytes 737304
  3.1 0.0 copy-start.2
  3.1 1.1 %copy-done.2 = bf16[5,64,1024]{2,1,0:T(8,128)(2,1)S(1)} copy-done((bf16[5,64,1024]{2,1,0:T(8,128)(2,1)S(1)}, bf16[5,64,1024]{2,1,0:T(8,128)(2,1)}, u32[]{:S(2)}) %copy-start.2) | copy-done | bytes 655384
  4.1 0.0 copy-start.3
  4.1 0.8 %copy-done.3 = bf16[128,256]{1,0:T(8,128)(2,1)S(1)} copy-done((bf16[128,256]{1,0:T(8,128)(2,1)S(1)}, bf16[128,256]{1,0:T(8,128)(2,1)}, u32[]{:S(2)}) %copy-start.3) | copy-done | bytes 65560
  5.0 0.0 copy-start.4
  5.0 0.8 %copy-done.4 = bf16[128,256]{1,0:T(8,128)(2,1)S(1)} copy-done((bf16[128,256]{1,0:T(8,128)(2,1)S(1)}, bf16[128,256]{1,0:T(8,128)(2,1)}, u32[]{:S(2)}) %copy-start.4) | copy-done | bytes 65560
  5.8 0.0 copy-start.5
  5.8 0.8 %copy-done.5 = bf16[128,256]{1,0:T(8,128)(2,1)S(1)} copy-done((bf16[128,256]{1,0:T(8,128)(2,1)S(1)}, bf16[128,256]{1,0:T(8,128)(2,1)}, u32[]{:S(2)}) %copy-start.5) | copy-done | bytes 65560
  6.7 0.0 copy-start.6
  6.7 0.8 %copy-done.6 = bf16[128,256]{1,0:T(8,128)(2,1)S(1)} copy-done((bf16[128,256]{1,0:T(8,128)(2,1)S(1)}, bf16[128,256]{1,0:T(8,128)(2,1)}, u32[]{:S(2)}) %copy-start.6) | copy-done | bytes 65560
  7.5 56.2 %shard_map.91 = bf16[64,256]{1,0:T(8,128)(2,1)S(1)} custom-call(bf16[5,64,1024]{2,1,0:T(8,128)(2,1)S(1)} %copy-done.2, bf16[1440,256]{1,0:T(8,128)(2,1)S(1)} %copy-done.1, bf16[1,1024]{1,0:T(2,128)(2,1)S(1)} %reshape.6.token_gain_ref, bf16[512,1024]{1,0:T(8,128)(2,1)S(1)} %copy-done, bf16[1,1024]{1,0:T(2,128)(2,1)S(1)} %reshape.7.latent_gain_ref, ...), custom_call_target="tpu_custom_call" | custom-call | tf_op jit(solution)/shard_map/pallas_call | solution.py:569
  63.8 0.6 copy.11
  (1 shorter events, 0.0 us)
Async XLA Ops:
  0.0 0.7 %copy-start.7 = (bf16[1024]{0:T(1024)(128)(2,1)S(1)}, bf16[1024]{0:T(1024)(128)(2,1)}, u32[]{:S(2)}) copy-start(bf16[1024]{0:T(1024)(128)(2,1)} %param.13) | copy-start | bytes 6148
  0.7 1.2 %copy-start = (bf16[512,1024]{1,0:T(8,128)(2,1)S(1)}, bf16[512,1024]{1,0:T(8,128)(2,1)}, u32[]{:S(2)}) copy-start(bf16[512,1024]{1,0:T(8,128)(2,1)} %latents_ref.1) | copy-start | bytes 3145732
  1.9 1.1 %copy-start.1 = (bf16[1440,256]{1,0:T(8,128)(2,1)S(1)}, bf16[1440,256]{1,0:T(8,128)(2,1)}, u32[]{:S(2)}) copy-start(bf16[1440,256]{1,0:T(8,128)(2,1)} %stem_ref.1) | copy-start | bytes 2211844
  3.1 1.1 %copy-start.2 = (bf16[5,64,1024]{2,1,0:T(8,128)(2,1)S(1)}, bf16[5,64,1024]{2,1,0:T(8,128)(2,1)}, u32[]{:S(2)}) copy-start(bf16[5,64,1024]{2,1,0:T(8,128)(2,1)} %image_ref.1) | copy-start | bytes 1966084
  4.1 0.8 %copy-start.3 = (bf16[128,256]{1,0:T(8,128)(2,1)S(1)}, bf16[128,256]{1,0:T(8,128)(2,1)}, u32[]{:S(2)}) copy-start(bf16[128,256]{1,0:T(8,128)(2,1)} %wq_ref.1) | copy-start | bytes 196612
  5.0 0.8 %copy-start.4 = (bf16[128,256]{1,0:T(8,128)(2,1)S(1)}, bf16[128,256]{1,0:T(8,128)(2,1)}, u32[]{:S(2)}) copy-start(bf16[128,256]{1,0:T(8,128)(2,1)} %wk_ref.1) | copy-start | bytes 196612
  5.8 0.8 %copy-start.5 = (bf16[128,256]{1,0:T(8,128)(2,1)S(1)}, bf16[128,256]{1,0:T(8,128)(2,1)}, u32[]{:S(2)}) copy-start(bf16[128,256]{1,0:T(8,128)(2,1)} %wv_ref.1) | copy-start | bytes 196612
  6.7 0.8 %copy-start.6 = (bf16[128,256]{1,0:T(8,128)(2,1)S(1)}, bf16[128,256]{1,0:T(8,128)(2,1)}, u32[]{:S(2)}) copy-start(bf16[128,256]{1,0:T(8,128)(2,1)} %wo_ref.1) | copy-start | bytes 196612

commit v3 on v2

--- a/solution.py
+++ b/solution.py
@@ -136,6 +136,10 @@
     return lax.broadcasted_iota(jnp.int32, shape, dim)
 
 
+def over(index, power):
+    return lax.shift_right_logical(index, power.bit_length() - 1)
+
+
 def band_and_line(flat):
     band = jnp.zeros_like(flat)
     for step in range(1, BANDS + 1):
@@ -158,6 +162,8 @@
     out_ref,
     image,
     stem,
+    token_gain,
+    latent_gain,
     latent_rows,
     latent_norm,
     query_part,
@@ -166,8 +172,7 @@
     lines_in,
     wide,
     order,
-    ordered,
-    stem_sum,
+    left,
     part_out,
     part_in,
     feature,
@@ -228,6 +233,8 @@
                     latents_ref.at[pl.ds(pl.multiple_of(z * 2 * own, 2 * own), 2 * own)],
                     latent_rows,
                 ),
+                (token_gain_ref, token_gain),
+                (latent_gain_ref, latent_gain),
             ]
         )
     ]
@@ -244,16 +251,21 @@
             barrier, inc=1, device_id=(r, lax.rem(h + d, heads)), device_id_type=MESH
         )
 
-    slots = rows * 2 * pad
-    row = iota((slots, 1), 0)
-    receiver, second, line = row // (2 * pad), (row // pad) % 2, row % pad
-    band, at = band_and_line(per * receiver + line)
+    quarter = pad // 2
     height = image_ref.shape[1]
-    source = band * height + jnp.where(second == 1, (at + STRIDE) % height, at)
-    pick = (iota((slots, BANDS * height), 1) == source).astype(BF16)
+
+    def pick(receiver, second, line):
+        band, at = band_and_line(per * receiver + line)
+        source = band * height + ((at + STRIDE * second) & (height - 1))
+        places = iota((source.shape[0], BANDS * height), 1)
+        flat = image[...].reshape(BANDS * height, pixels)
+        return dot((places == source).astype(BF16), flat).astype(BF16)
+
+    row = iota((rows * quarter, 1), 0)
     loads[0].wait()
-    flat = image[...].reshape(BANDS * height, pixels)
-    lines_out[...] = dot(pick, flat).astype(BF16).reshape(lines_out.shape)
+    lines_out[...] = pick(over(row, quarter), core, half * quarter + (row & (quarter - 1))).reshape(
+        lines_out.shape
+    )
     pl.semaphore_wait(barrier, rows - 1 + heads - 1)
 
     def remote(src, dst, send, recv, to):
@@ -274,14 +286,14 @@
             remote(
                 buf.at[r],
                 buf.at[r],
-                gz_s.at[d],
-                gz_r.at[d],
+                gz_s.at[which, d],
+                gz_r.at[which, d],
                 (lax.rem(r + 2 * d, rows), h),
             )
             for d in range(1, rows // 2)
         ]
         across = remote(
-            buf.at[r], buf.at[r], gy_s.at[which, 0], gy_r.at[which, 0], (y_peer, h)
+            buf.at[r], buf.at[r], gy_s.at[2 + which, 0], gy_r.at[2 + which, 0], (y_peer, h)
         )
         return first, [across]
 
@@ -294,8 +306,8 @@
                 remote(
                     buf.at[slot],
                     buf.at[slot],
-                    gy_s.at[which, d],
-                    gy_r.at[which, d],
+                    gy_s.at[2 + which, d],
+                    gy_r.at[2 + which, d],
                     (y_peer, h),
                 )
             )
@@ -333,24 +345,24 @@
     def second_only(buf, slot):
         return buf.at[slot, 1]
 
-    quarter = pad // 2
-
     def lines_at(ref, slot, part):
         return ref.at[slot, core, pl.ds(pl.multiple_of(part * quarter, quarter), quarter)]
 
+    far_first = (4, 3, 5, 2, 6, 1, 7)
     line_copies = []
-    for d in range(1, rows):
+    for d in far_first:
         to = lax.rem(r + d, rows)
         line_copies.append(
             remote(
-                lines_at(lines_out, to, half),
+                lines_out.at[to],
                 lines_at(lines_in, r, half),
                 line_s.at[0, d],
                 line_r.at[0, d],
                 (to, h),
             )
         )
-    lines_in[r] = lines_out[r]
+    row = iota((2 * pad, 1), 0)
+    lines_in[r] = pick(r, over(row, pad), row & (pad - 1)).reshape(2, pad, pixels)
     loads[1].wait()
     loads[2].wait()
 
@@ -380,10 +392,10 @@
 
     token_rows = rows * TROWS
     row = iota((per * token_rows, 1), 0)
-    line, token_row = row // token_rows, row % token_rows
+    line, token_row = over(row, token_rows), row & (token_rows - 1)
     _, at = band_and_line(per * r + line)
-    odd = token_row % 2
-    strip = token_row // 2 + jnp.where((odd == 1) & (at >= STRIDE), 1, 0)
+    odd = token_row & 1
+    strip = over(token_row, 2) + jnp.where((odd == 1) & (at >= STRIDE), 1, 0)
     target = (strip * 2 + odd) * pad + line
     order[...] = (iota(order.shape, 1) == target).astype(BF16)
 
@@ -392,12 +404,12 @@
         return remote(ref, ref, line_s.at[k, d], line_r.at[k, d], (r, to))
 
     over_x, over_core = [], []
-    for d, copy in enumerate(line_copies, 1):
+    for d, copy in zip(far_first, line_copies):
         copy.wait_recv()
         slot = lax.rem(r + rows - d, rows)
         over_x.append(pass_line(slot, half, 1, d, x_peer))
         over_core.append(pass_line(slot, half, 2, d, core_peer))
-    for d, copy in enumerate(over_x, 1):
+    for d, copy in zip(far_first, over_x):
         copy.wait_recv()
         slot = lax.rem(r + rows - d, rows)
         over_core.append(pass_line(slot, 1 - half, 3, d, core_peer))
@@ -406,70 +418,62 @@
     second_state = z_start(w_second, 1, second_only)
     for copy in over_core:
         copy.wait_recv()
-    ordered[...] = dot(order[...], lines_in[...].reshape(slots, pixels)).astype(BF16)
-
+    lines = dot(order[...], lines_in[...].reshape(rows * 2 * pad, pixels)).astype(BF16)
+    for f in range(per):
+        for g in range(groups):
+            left[g * token_rows : (g + 1) * token_rows, 128 * f : 128 * f + 128] = lines[
+                f * token_rows : (f + 1) * token_rows, 128 * g : 128 * g + 128
+            ]
     z_pass(w_first, 0, whole_slot, first_state)
 
-    at_once = 6
-    stem_sum[...] = jnp.zeros_like(stem_sum)
-
-    def stem_step(step, carry):
-        blocks = []
-        for k in range(at_once):
-            f = step * at_once + k
-            x = ordered[pl.ds(pl.multiple_of(f * token_rows, 16), token_rows), :]
-            blocks.append(
-                jnp.concatenate([x[:, 128 * g : 128 * g + 128] for g in range(groups)], axis=0)
-            )
-        left = jnp.concatenate(blocks, axis=1)
-        depth = at_once * 128
-        stem_sum[...] += dot(left, wide[pl.ds(pl.multiple_of(step * depth, 128), depth), :])
-        return carry
-
-    lax.fori_loop(0, per // at_once, stem_step, 0)
-    last = VARIANTS - 2
-    rim = jnp.concatenate(
-        [
-            stem_sum[token_rows:, (last + 1) * width :],
-            jnp.zeros((token_rows, width), F32),
-        ],
-        axis=0,
-    )
-    sums = jnp.concatenate(
-        [
-            stem_sum[:, : last * width],
-            stem_sum[:, last * width : (last + 1) * width] + rim,
-        ],
-        axis=1,
-    ).astype(BF16)
     each = groups * TROWS
     row = iota((rows * each, 1), 0)
-    strip, group, inner = row // each, (row % each) // TROWS, row % TROWS
+    strip, group, inner = over(row, each), over(row & (each - 1), TROWS), row & (TROWS - 1)
     turn = iota((rows * each, rows * each), 1) == group * token_rows + strip * TROWS + inner
-    part_out[...] = dot(turn.astype(BF16), sums).astype(BF16).reshape(part_out.shape)
-
+    turn = turn.astype(BF16)
     part_copies = []
-    for d in range(1, rows):
-        to = lax.rem(r + d, rows)
-        part_copies.append(
-            remote(part_out.at[to], part_in.at[r], part_s.at[d], part_r.at[d], (to, h))
-        )
-    part_in[r] = part_out[r]
+
+    def send_sums(k, sums):
+        sums = jnp.concatenate(sums, axis=1).astype(BF16)
+        part_out[k] = dot(turn, sums).astype(BF16).reshape(part_out.shape[1:])
+        for d in far_first:
+            to = lax.rem(r + d, rows)
+            part_copies.append(
+                remote(
+                    part_out.at[k, to],
+                    part_in.at[k, r],
+                    part_s.at[k, d],
+                    part_r.at[k, d],
+                    (to, h),
+                )
+            )
+        part_in[k, r] = part_out[k, r]
+
+    def stem_dot(v):
+        return dot(left[...], wide[:, v * width : (v + 1) * width])
+
+    send_sums(0, [stem_dot(0), stem_dot(1)])
+    rim = stem_dot(4)
+    rim = jnp.concatenate([rim[token_rows:], jnp.zeros((token_rows, width), F32)], axis=0)
+    send_sums(1, [stem_dot(2), stem_dot(3) + rim])
 
     def norm(x, gain_ref):
         average = jnp.mean(x, axis=-1, keepdims=True)
         centered = x - average
         variance = jnp.mean(centered * centered, axis=-1, keepdims=True)
-        return (centered * lax.rsqrt(variance + epsilon) * gain_ref[...].astype(F32)).astype(BF16)
+        return (centered * lax.rsqrt(variance + epsilon) * gain_ref[...].astype(F32).reshape(1, -1)).astype(
+            BF16
+        )
 
     z_end(w_first, 0, whole_slot, first_state)
-    loads[6].wait()
-    latent_norm[...] = norm(latent_rows[...].astype(F32), latent_gain_ref)
+    for copy in loads[6:]:
+        copy.wait()
+    latent_norm[...] = norm(latent_rows[...].astype(F32), latent_gain)
     for copy in part_copies:
         copy.wait_recv()
-    total = jnp.sum(part_in[...].astype(F32), axis=0)
+    total = jnp.sum(part_in[...].astype(F32), axis=1)
     feature[h] = jnp.concatenate(
-        [total[:, v * width : (v + 1) * width] for v in range(last + 1)], axis=0
+        [total[k, :, v * width : (v + 1) * width] for k in range(2) for v in range(2)], axis=0
     ).astype(BF16)
 
     feat_copies = []
@@ -488,12 +492,12 @@
     for copy in feat_copies:
         copy.wait_recv()
     token_norm = norm(
-        jnp.concatenate([feature[k] for k in range(heads)], axis=1).astype(F32), token_gain_ref
-    )
+        jnp.concatenate([feature[k] for k in range(heads)], axis=1).astype(F32), token_gain
+    )
+    kv_states = []
     for k in range(2):
-        kv[r, k] = dot(token_norm, w_first[:, k].reshape(D, width)).astype(BF16)
-    kv_state = gather_start(kv, 2)
-
+        kv[k, r] = dot(token_norm, w_first[:, k].reshape(D, width)).astype(BF16)
+        kv_states.append(gather_start(kv.at[k], k))
     z_end(w_second, 1, second_only, second_state)
     depth = wq_ref.shape[0]
     part = jnp.zeros((2 * own, width), F32)
@@ -504,32 +508,37 @@
         )
     query_part[...] = part.reshape(query_part.shape)
     query_copy = remote(query_part.at[1 - y], query_in, query_s, query_r, (y_peer, h))
-    gather_forward(kv, 2, kv_state)
+    gather_forward(kv.at[0], 0, kv_states[0])
     query_copy.wait_recv()
     queries = (query_part[y] + query_in[...]).astype(BF16)
-    gather_wait(kv_state)
-
-    tokens = kv.shape[0] * kv.shape[2]
-    keys = kv[:, 0].reshape(tokens, width)
-    values = kv[:, 1].reshape(tokens, width)
+    gather_wait(kv_states[0])
+
+    tokens = rows * kv.shape[2]
+    keys = kv[0].reshape(tokens, width)
     size = D // HEADS
+    side = iota((own, 128), 1) < size
+    weights, totals = [], []
+    for pair in range(width // 128):
+        cols = slice(128 * pair, 128 * pair + 128)
+        for keep in (side, jnp.logical_not(side)):
+            mine = jnp.where(keep, queries[:, cols].astype(F32), 0.0).astype(BF16)
+            scores = lax.dot_general(
+                mine, keys[:, cols], (((1,), (1,)), ((), ())), preferred_element_type=F32
+            ) * size ** (-0.5)
+            weight = jnp.exp(scores - jnp.max(scores, axis=1, keepdims=True))
+            weights.append(weight)
+            totals.append(jnp.sum(weight, axis=1, keepdims=True))
+    gather_forward(kv.at[1], 1, kv_states[1])
+    gather_wait(kv_states[1])
+    values = kv[1].reshape(tokens, width)
     mixed = []
     for pair in range(width // 128):
-        cols = slice(128 * pair, 128 * pair + 128)
-        q, k, v = queries[:, cols], keys[:, cols], values[:, cols]
-        side = iota((own, 128), 1) < size
+        v = values[:, 128 * pair : 128 * pair + 128]
         halves = []
-        for low in (True, False):
-            keep = side if low else jnp.logical_not(side)
-            mine = jnp.where(keep, q.astype(F32), 0.0).astype(BF16)
-            scores = lax.dot_general(
-                mine, k, (((1,), (1,)), ((), ())), preferred_element_type=F32
-            ) * size ** (-0.5)
-            weights = jnp.exp(scores - jnp.max(scores, axis=1, keepdims=True))
-            totals = jnp.sum(weights, axis=1, keepdims=True)
-            upper = weights.astype(BF16)
-            lower = (weights - upper.astype(F32)).astype(BF16)
-            halves.append((dot(upper, v) + dot(lower, v)) / totals)
+        for k in (2 * pair, 2 * pair + 1):
+            upper = weights[k].astype(BF16)
+            lower = (weights[k] - upper.astype(F32)).astype(BF16)
+            halves.append((dot(upper, v) + dot(lower, v)) / totals[k])
         mixed.append(jnp.where(side, halves[0], halves[1]).astype(BF16))
     mixed = jnp.concatenate(mixed, axis=1)
 
@@ -569,59 +578,57 @@
         return pl.pallas_call(
             functools.partial(strip_kernel, rows, heads),
             out_shape=jax.ShapeDtypeStruct((own, width), BF16),
-            in_specs=[
-                pl.BlockSpec(memory_space=pltpu.VMEM if k in (2, 4) else pltpu.HBM)
-                for k in range(9)
-            ],
+            in_specs=[pl.BlockSpec(memory_space=pltpu.HBM)] * 9,
             out_specs=pl.BlockSpec(memory_space=pltpu.VMEM),
             scratch_shapes=[
                 pltpu.VMEM(imagery.shape, BF16),
                 pltpu.VMEM(stem.shape, BF16),
+                pltpu.VMEM((D,), BF16),
+                pltpu.VMEM((D,), BF16),
                 pltpu.VMEM((2 * own, D), BF16),
                 pltpu.VMEM((2 * own, D), BF16),
                 pltpu.VMEM((2, own, width), F32),
                 pltpu.VMEM((own, width), F32),
-                pltpu.VMEM((rows, 2, pad, pixels), BF16),
+                pltpu.VMEM((rows, pad // 2, pixels), BF16),
                 pltpu.VMEM((rows, 2, pad, pixels), BF16),
                 pltpu.VMEM((per * 128, VARIANTS * width), BF16),
                 pltpu.VMEM((per * token_rows, rows * 2 * pad), BF16),
-                pltpu.VMEM((per * token_rows, pixels), BF16),
-                pltpu.VMEM((groups * token_rows, VARIANTS * width), F32),
-                pltpu.VMEM((rows, groups * TROWS, 4 * width), BF16),
-                pltpu.VMEM((rows, groups * TROWS, 4 * width), BF16),
+                pltpu.VMEM((groups * token_rows, per * 128), BF16),
+                pltpu.VMEM((2, rows, groups * TROWS, 2 * width), BF16),
+                pltpu.VMEM((2, rows, groups * TROWS, 2 * width), BF16),
                 pltpu.VMEM((heads, tokens, width), BF16),
                 pltpu.VMEM((rows, 2, wk.shape[0], width), BF16),
                 pltpu.VMEM((rows, 2, wk.shape[0], width), BF16),
-                pltpu.VMEM((rows, 2, tokens, width), BF16),
+                pltpu.VMEM((2, rows, tokens, width), BF16),
                 pltpu.VMEM((heads, own, width), F32),
                 pltpu.VMEM((heads - 1, own, width), F32),
-                dma((7,)),
+                dma((9,)),
                 dma((4, rows)),
                 dma((4, rows)),
                 dma,
                 dma,
-                dma((rows,)),
-                dma((rows,)),
+                dma((2, rows)),
+                dma((2, rows)),
                 dma((heads,)),
                 dma((heads,)),
                 dma((heads,)),
                 dma((heads,)),
                 dma((2, 3)),
                 dma((2, 3)),
-                dma((rows // 2,)),
-                dma((rows // 2,)),
-                dma((3, rows // 2)),
-                dma((3, rows // 2)),
+                dma((2, rows // 2)),
+                dma((2, rows // 2)),
+                dma((4, rows // 2)),
+                dma((4, rows // 2)),
             ],
             compiler_params=pltpu.CompilerParams(
-                collective_id=0, has_side_effects=True, vmem_limit_bytes=48 * 2**20
+                collective_id=0, has_side_effects=True, vmem_limit_bytes=60 * 2**20
             ),
         )(
             imagery,
             stem,
-            token_gain.reshape(1, -1),
+            token_gain,
             latents,
-            latent_gain.reshape(1, -1),
+            latent_gain,
             wq,
             wk,
             wv,

time: 64.8 us -> 58.7 us (0.906)
  local copies, waits for them, and re-layouts: 8.1 us -> 1.38 us
  Pallas kernels: 56.2 us -> 57 us
    unnamed x17 -> x1, local copies, waits for them, and re-layouts: 7.4 us -> 1.38 us
    pallas_call x1, Pallas kernels: 56.2 us -> 57 us  [per_chip(): pl.pallas_call(functools.partial(strip_kernel, rows, heads), out_shape=ja...]
    reshape x2 -> x0, local copies, waits for them, and re-layouts: 0.7 us -> none  [the longest x1 0.7 us: per_chip(): token_gain.reshape(1, -1)]
where the time goes in v3:
time: 58.7 us; the launch traced here: 58.4 us
  Pallas kernels  57 us (97%)
  local copies, waits for them, and re-layouts  1.38 us (2%)
    pallas_call x1, Pallas kernels, per_chip(): pl.pallas_call(functools.partial(strip_kernel, rows, heads), out_shape=ja...  57 us
    unnamed x1, local copies, waits for them, and re-layouts  1.38 us

profile of v3, /device:TPU:0, one launch (start us, length us, event | category | flops | bytes accessed | tf_op | source)
XLA Modules:
  0.0 58.4 jit_solution(413771683196426169)
XLA Ops:
  0.0 57.0 %shard_map.91 = bf16[64,256]{1,0:T(8,128)(2,1)} custom-call(bf16[5,64,1024]{2,1,0:T(8,128)(2,1)} %image_ref.1, bf16[1440,256]{1,0:T(8,128)(2,1)} %stem_ref.1, bf16[1024]{0:T(1024)(128)(2,1)} %token_gain_ref.1, bf16[512,1024]{1,0:T(8,128)(2,1)} %latents_ref.1, bf16[1024]{0:T(1024)(128)(2,1)} %latent_gain_ref.1, bf16[128,256]{1,0:T(8,128)(2,1)} %wq_ref.1, ...), custom_call_target="tpu_custom_call" | custom-call | tf_op jit(solution)/shard_map/pallas_call | solution.py:578
  57.0 1.4 %copy.11 = bf16[64,256]{1,0:T(8,128)(2,1)} copy(bf16[64,256]{1,0:T(8,128)(2,1)} %shard_map.91) | data formatting | bytes 65536

commit v4 on v3

--- a/solution.py
+++ b/solution.py
@@ -177,7 +177,8 @@
     part_in,
     feature,
     w_first,
-    w_second,
+    w_query,
+    w_out,
     kv,
     out_terms,
     out_in,
@@ -227,8 +228,8 @@
                 (wk_ref, w_first.at[r, 0]),
                 (wv_ref, w_first.at[r, 1]),
                 (stem_ref, stem),
-                (wq_ref, w_second.at[r, 0]),
-                (wo_ref, w_second.at[r, 1]),
+                (wq_ref, w_query.at[r]),
+                (wo_ref, w_out.at[r]),
                 (
                     latents_ref.at[pl.ds(pl.multiple_of(z * 2 * own, 2 * own), 2 * own)],
                     latent_rows,
@@ -262,6 +263,7 @@
         return dot((places == source).astype(BF16), flat).astype(BF16)
 
     row = iota((rows * quarter, 1), 0)
+    wide[...] = jnp.zeros_like(wide)
     loads[0].wait()
     lines_out[...] = pick(over(row, quarter), core, half * quarter + (row & (quarter - 1))).reshape(
         lines_out.shape
@@ -293,7 +295,7 @@
             for d in range(1, rows // 2)
         ]
         across = remote(
-            buf.at[r], buf.at[r], gy_s.at[2 + which, 0], gy_r.at[2 + which, 0], (y_peer, h)
+            buf.at[r], buf.at[r], gy_s.at[3 + which, 0], gy_r.at[3 + which, 0], (y_peer, h)
         )
         return first, [across]
 
@@ -306,8 +308,8 @@
                 remote(
                     buf.at[slot],
                     buf.at[slot],
-                    gy_s.at[2 + which, d],
-                    gy_r.at[2 + which, d],
+                    gy_s.at[3 + which, d],
+                    gy_r.at[3 + which, d],
                     (y_peer, h),
                 )
             )
@@ -316,34 +318,37 @@
         for copy in state[1]:
             copy.wait_recv()
 
-    def z_start(buf, which, part):
-        return [
+    def z_start(buf, which, over_y=True):
+        first = [
             remote(buf.at[r], buf.at[r], z_s.at[which, 0], z_r.at[which, 0], (z_opposite, h)),
             remote(buf.at[r], buf.at[r], z_s.at[which, 1], z_r.at[which, 1], (z_pair, h)),
-        ], [y_send(part(buf, r), which, 0)]
-
-    def y_send(ref, which, k):
-        return remote(ref, ref, gy_s.at[which, k], gy_r.at[which, k], (y_peer, h))
-
-    def z_pass(buf, which, part, state):
-        first, across = state
+        ]
+        across = []
+
+        def y_send(slot):
+            k = len(across)
+            if over_y:
+                ref = buf.at[slot]
+                across.append(
+                    remote(ref, ref, gy_s.at[which, k], gy_r.at[which, k], (y_peer, h))
+                )
+
+        y_send(r)
+        return buf, which, first, across, y_send
+
+    def z_pass(state):
+        buf, which, first, across, y_send = state
         first[0].wait_recv()
         ref = buf.at[z_opposite]
         first.append(remote(ref, ref, z_s.at[which, 2], z_r.at[which, 2], (z_pair, h)))
-        across.append(y_send(part(buf, z_opposite), which, 1))
+        y_send(z_opposite)
         first[1].wait_recv()
-        across.append(y_send(part(buf, z_pair), which, 2))
-
-    def z_end(buf, which, part, state):
-        first, across = state
+        y_send(z_pair)
+
+    def z_end(state):
+        buf, which, first, across, y_send = state
         first[2].wait_recv()
-        across.append(y_send(part(buf, z_last), which, 3))
-
-    def whole_slot(buf, slot):
-        return buf.at[slot]
-
-    def second_only(buf, slot):
-        return buf.at[slot, 1]
+        y_send(z_last)
 
     def lines_at(ref, slot, part):
         return ref.at[slot, core, pl.ds(pl.multiple_of(part * quarter, quarter), quarter)]
@@ -363,13 +368,6 @@
         )
     row = iota((2 * pad, 1), 0)
     lines_in[r] = pick(r, over(row, pad), row & (pad - 1)).reshape(2, pad, pixels)
-    loads[1].wait()
-    loads[2].wait()
-
-    wide[...] = jnp.zeros_like(wide)
-    first_state = z_start(w_first, 0, whole_slot)
-    loads[3].wait()
-
     def widen(f, carry):
         block = stem[pl.ds(pl.multiple_of(f * KER, 16), KER), :]
         for v in range(VARIANTS - 2):
@@ -388,8 +386,6 @@
         ] = block[STRIDE:]
         return carry
 
-    lax.fori_loop(0, per, widen, 0)
-
     token_rows = rows * TROWS
     row = iota((per * token_rows, 1), 0)
     line, token_row = over(row, token_rows), row & (token_rows - 1)
@@ -404,18 +400,21 @@
         return remote(ref, ref, line_s.at[k, d], line_r.at[k, d], (r, to))
 
     over_x, over_core = [], []
-    for d, copy in zip(far_first, line_copies):
+    loads[3].wait()
+    parts = len(far_first)
+    for k, (d, copy) in enumerate(zip(far_first, line_copies)):
+        lax.fori_loop(per * k // parts, per * (k + 1) // parts, widen, 0)
         copy.wait_recv()
         slot = lax.rem(r + rows - d, rows)
         over_x.append(pass_line(slot, half, 1, d, x_peer))
         over_core.append(pass_line(slot, half, 2, d, core_peer))
+    loads[1].wait()
+    loads[2].wait()
+    first_state = z_start(w_first, 0)
     for d, copy in zip(far_first, over_x):
         copy.wait_recv()
         slot = lax.rem(r + rows - d, rows)
         over_core.append(pass_line(slot, 1 - half, 3, d, core_peer))
-    loads[4].wait()
-    loads[5].wait()
-    second_state = z_start(w_second, 1, second_only)
     for copy in over_core:
         copy.wait_recv()
     lines = dot(order[...], lines_in[...].reshape(rows * 2 * pad, pixels)).astype(BF16)
@@ -424,7 +423,7 @@
             left[g * token_rows : (g + 1) * token_rows, 128 * f : 128 * f + 128] = lines[
                 f * token_rows : (f + 1) * token_rows, 128 * g : 128 * g + 128
             ]
-    z_pass(w_first, 0, whole_slot, first_state)
+    z_pass(first_state)
 
     each = groups * TROWS
     row = iota((rows * each, 1), 0)
@@ -456,6 +455,8 @@
     rim = stem_dot(4)
     rim = jnp.concatenate([rim[token_rows:], jnp.zeros((token_rows, width), F32)], axis=0)
     send_sums(1, [stem_dot(2), stem_dot(3) + rim])
+    loads[4].wait()
+    query_state = z_start(w_query, 1, over_y=False)
 
     def norm(x, gain_ref):
         average = jnp.mean(x, axis=-1, keepdims=True)
@@ -465,7 +466,7 @@
             BF16
         )
 
-    z_end(w_first, 0, whole_slot, first_state)
+    z_end(first_state)
     for copy in loads[6:]:
         copy.wait()
     latent_norm[...] = norm(latent_rows[...].astype(F32), latent_gain)
@@ -487,8 +488,10 @@
                 (r, lax.rem(h + d, heads)),
             )
         )
-    z_pass(w_second, 1, second_only, second_state)
-    gather_wait(first_state)
+    loads[5].wait()
+    out_state = z_start(w_out, 2)
+    z_pass(query_state)
+    gather_wait(first_state[2:])
     for copy in feat_copies:
         copy.wait_recv()
     token_norm = norm(
@@ -498,16 +501,17 @@
     for k in range(2):
         kv[k, r] = dot(token_norm, w_first[:, k].reshape(D, width)).astype(BF16)
         kv_states.append(gather_start(kv.at[k], k))
-    z_end(w_second, 1, second_only, second_state)
+    z_end(query_state)
     depth = wq_ref.shape[0]
     part = jnp.zeros((2 * own, width), F32)
     for k in range(rows // 2):
         at = 2 * k + y
         part = part + dot(
-            latent_norm[:, pl.ds(pl.multiple_of(at * depth, depth), depth)], w_second[at, 0]
+            latent_norm[:, pl.ds(pl.multiple_of(at * depth, depth), depth)], w_query[at]
         )
     query_part[...] = part.reshape(query_part.shape)
     query_copy = remote(query_part.at[1 - y], query_in, query_s, query_r, (y_peer, h))
+    z_pass(out_state)
     gather_forward(kv.at[0], 0, kv_states[0])
     query_copy.wait_recv()
     queries = (query_part[y] + query_in[...]).astype(BF16)
@@ -529,6 +533,7 @@
             weights.append(weight)
             totals.append(jnp.sum(weight, axis=1, keepdims=True))
     gather_forward(kv.at[1], 1, kv_states[1])
+    z_end(out_state)
     gather_wait(kv_states[1])
     values = kv[1].reshape(tokens, width)
     mixed = []
@@ -542,10 +547,10 @@
         mixed.append(jnp.where(side, halves[0], halves[1]).astype(BF16))
     mixed = jnp.concatenate(mixed, axis=1)
 
-    gather_wait(second_state)
+    gather_wait(out_state[2:])
     for k in range(heads):
-        per_head = w_second.shape[0] // heads
-        block = w_second[per_head * k : per_head * (k + 1), 1].reshape(width, width)
+        per_head = w_out.shape[0] // heads
+        block = w_out[per_head * k : per_head * (k + 1)].reshape(width, width)
         out_terms[k] = lax.dot_general(
             mixed, block, (((1,), (1,)), ((), ())), preferred_element_type=F32
         )
@@ -598,7 +603,8 @@
                 pltpu.VMEM((2, rows, groups * TROWS, 2 * width), BF16),
                 pltpu.VMEM((heads, tokens, width), BF16),
                 pltpu.VMEM((rows, 2, wk.shape[0], width), BF16),
-                pltpu.VMEM((rows, 2, wk.shape[0], width), BF16),
+                pltpu.VMEM((rows, wq.shape[0], width), BF16),
+                pltpu.VMEM((rows, wo.shape[0], width), BF16),
                 pltpu.VMEM((2, rows, tokens, width), BF16),
                 pltpu.VMEM((heads, own, width), F32),
                 pltpu.VMEM((heads - 1, own, width), F32),
@@ -613,12 +619,12 @@
                 dma((heads,)),
                 dma((heads,)),
                 dma((heads,)),
-                dma((2, 3)),
-                dma((2, 3)),
+                dma((3, 3)),
+                dma((3, 3)),
                 dma((2, rows // 2)),
                 dma((2, rows // 2)),
-                dma((4, rows // 2)),
-                dma((4, rows // 2)),
+                dma((5, rows // 2)),
+                dma((5, rows // 2)),
             ],
             compiler_params=pltpu.CompilerParams(
                 collective_id=0, has_side_effects=True, vmem_limit_bytes=60 * 2**20

time: 58.7 us -> 57.4 us (0.978)
  Pallas kernels: 57 us -> 55.8 us
    pallas_call x1, Pallas kernels: 57 us -> 55.8 us  [per_chip(): pl.pallas_call(functools.partial(strip_kernel, rows, heads), out_shape=ja...]
where the time goes in v4:
time: 57.4 us; the launch traced here: 57.2 us
  Pallas kernels  55.8 us (97%)
  local copies, waits for them, and re-layouts  1.38 us (2%)
    pallas_call x1, Pallas kernels, per_chip(): pl.pallas_call(functools.partial(strip_kernel, rows, heads), out_shape=ja...  55.8 us
    unnamed x1, local copies, waits for them, and re-layouts  1.38 us

profile of v4, /device:TPU:0, one launch (start us, length us, event | category | flops | bytes accessed | tf_op | source)
XLA Modules:
  0.0 57.2 jit_solution(14314499799664319726)
XLA Ops:
  0.0 55.8 %shard_map.91 = bf16[64,256]{1,0:T(8,128)(2,1)} custom-call(bf16[5,64,1024]{2,1,0:T(8,128)(2,1)} %image_ref.1, bf16[1440,256]{1,0:T(8,128)(2,1)} %stem_ref.1, bf16[1024]{0:T(1024)(128)(2,1)} %token_gain_ref.1, bf16[512,1024]{1,0:T(8,128)(2,1)} %latents_ref.1, bf16[1024]{0:T(1024)(128)(2,1)} %latent_gain_ref.1, bf16[128,256]{1,0:T(8,128)(2,1)} %wq_ref.1, ...), custom_call_target="tpu_custom_call" | custom-call | tf_op jit(solution)/shard_map/pallas_call | solution.py:583
  55.8 1.4 %copy.11 = bf16[64,256]{1,0:T(8,128)(2,1)} copy(bf16[64,256]{1,0:T(8,128)(2,1)} %shard_map.91) | data formatting | bytes 65536

commit v5 on v4

--- a/solution.py
+++ b/solution.py
@@ -173,6 +173,7 @@
     wide,
     order,
     left,
+    stem_sum,
     part_out,
     part_in,
     feature,
@@ -214,7 +215,7 @@
     z_last = lax.rem(z_pair + 4, rows)
     own = latents_ref.shape[0] // rows
     per = stem_ref.shape[0] // KER
-    pad = lines_in.shape[2]
+    quarter = lines_in.shape[3]
     width = stem_ref.shape[1]
     pixels = image_ref.shape[2]
     groups = pixels // 128
@@ -252,7 +253,6 @@
             barrier, inc=1, device_id=(r, lax.rem(h + d, heads)), device_id_type=MESH
         )
 
-    quarter = pad // 2
     height = image_ref.shape[1]
 
     def pick(receiver, second, line):
@@ -350,9 +350,6 @@
         first[2].wait_recv()
         y_send(z_last)
 
-    def lines_at(ref, slot, part):
-        return ref.at[slot, core, pl.ds(pl.multiple_of(part * quarter, quarter), quarter)]
-
     far_first = (4, 3, 5, 2, 6, 1, 7)
     line_copies = []
     for d in far_first:
@@ -360,14 +357,17 @@
         line_copies.append(
             remote(
                 lines_out.at[to],
-                lines_at(lines_in, r, half),
+                lines_in.at[half, r, core],
                 line_s.at[0, d],
                 line_r.at[0, d],
                 (to, h),
             )
         )
-    row = iota((2 * pad, 1), 0)
-    lines_in[r] = pick(r, over(row, pad), row & (pad - 1)).reshape(2, pad, pixels)
+    for part in range(2):
+        row = iota((2 * quarter, 1), 0)
+        lines_in[part, r] = pick(
+            r, over(row, quarter), part * quarter + (row & (quarter - 1))
+        ).reshape(2, quarter, pixels)
     def widen(f, carry):
         block = stem[pl.ds(pl.multiple_of(f * KER, 16), KER), :]
         for v in range(VARIANTS - 2):
@@ -387,16 +387,17 @@
         return carry
 
     token_rows = rows * TROWS
-    row = iota((per * token_rows, 1), 0)
+    row = iota((quarter * token_rows, 1), 0)
     line, token_row = over(row, token_rows), row & (token_rows - 1)
-    _, at = band_and_line(per * r + line)
     odd = token_row & 1
-    strip = over(token_row, 2) + jnp.where((odd == 1) & (at >= STRIDE), 1, 0)
-    target = (strip * 2 + odd) * pad + line
-    order[...] = (iota(order.shape, 1) == target).astype(BF16)
+    for part in range(2):
+        _, at = band_and_line(per * r + part * quarter + line)
+        strip = over(token_row, 2) + jnp.where((odd == 1) & (at >= STRIDE), 1, 0)
+        target = (strip * 2 + odd) * quarter + line
+        order[part] = (iota(order.shape[1:], 1) == target).astype(BF16)
 
     def pass_line(slot, part, k, d, to):
-        ref = lines_at(lines_in, slot, part)
+        ref = lines_in.at[part, slot, core]
         return remote(ref, ref, line_s.at[k, d], line_r.at[k, d], (r, to))
 
     over_x, over_core = [], []
@@ -411,18 +412,35 @@
     loads[1].wait()
     loads[2].wait()
     first_state = z_start(w_first, 0)
+    def order_lines(part):
+        lines = dot(
+            order[part], lines_in[part].reshape(rows * 2 * quarter, pixels)
+        ).astype(BF16)
+        for f in range(quarter):
+            for g in range(groups):
+                left[g * token_rows : (g + 1) * token_rows, 128 * f : 128 * f + 128] = lines[
+                    f * token_rows : (f + 1) * token_rows, 128 * g : 128 * g + 128
+                ]
+
+    depth = quarter * 128
+
+    def stem_dot(part, v):
+        at = pl.ds(pl.multiple_of(part * depth, depth), depth)
+        return dot(left[...], wide[at, v * width : (v + 1) * width])
+
+    for copy in over_core:
+        copy.wait_recv()
+    order_lines(half)
+    last_lines = []
     for d, copy in zip(far_first, over_x):
         copy.wait_recv()
         slot = lax.rem(r + rows - d, rows)
-        over_core.append(pass_line(slot, 1 - half, 3, d, core_peer))
-    for copy in over_core:
+        last_lines.append(pass_line(slot, 1 - half, 3, d, core_peer))
+    for v in range(VARIANTS):
+        stem_sum[:, v * width : (v + 1) * width] = stem_dot(half, v)
+    for copy in last_lines:
         copy.wait_recv()
-    lines = dot(order[...], lines_in[...].reshape(rows * 2 * pad, pixels)).astype(BF16)
-    for f in range(per):
-        for g in range(groups):
-            left[g * token_rows : (g + 1) * token_rows, 128 * f : 128 * f + 128] = lines[
-                f * token_rows : (f + 1) * token_rows, 128 * g : 128 * g + 128
-            ]
+    order_lines(1 - half)
     z_pass(first_state)
 
     each = groups * TROWS
@@ -448,13 +466,13 @@
             )
         part_in[k, r] = part_out[k, r]
 
-    def stem_dot(v):
-        return dot(left[...], wide[:, v * width : (v + 1) * width])
-
-    send_sums(0, [stem_dot(0), stem_dot(1)])
-    rim = stem_dot(4)
+    def both(v):
+        return stem_sum[:, v * width : (v + 1) * width] + stem_dot(1 - half, v)
+
+    send_sums(0, [both(0), both(1)])
+    rim = both(4)
     rim = jnp.concatenate([rim[token_rows:], jnp.zeros((token_rows, width), F32)], axis=0)
-    send_sums(1, [stem_dot(2), stem_dot(3) + rim])
+    send_sums(1, [both(2), both(3) + rim])
     loads[4].wait()
     query_state = z_start(w_query, 1, over_y=False)
 
@@ -524,14 +542,17 @@
     weights, totals = [], []
     for pair in range(width // 128):
         cols = slice(128 * pair, 128 * pair + 128)
-        for keep in (side, jnp.logical_not(side)):
-            mine = jnp.where(keep, queries[:, cols].astype(F32), 0.0).astype(BF16)
-            scores = lax.dot_general(
-                mine, keys[:, cols], (((1,), (1,)), ((), ())), preferred_element_type=F32
-            ) * size ** (-0.5)
-            weight = jnp.exp(scores - jnp.max(scores, axis=1, keepdims=True))
-            weights.append(weight)
-            totals.append(jnp.sum(weight, axis=1, keepdims=True))
+        q = queries[:, cols].astype(F32)
+        mine = jnp.concatenate([jnp.where(side, q, 0.0), jnp.where(side, 0.0, q)], axis=0)
+        scores = lax.dot_general(
+            mine.astype(BF16),
+            keys[:, cols],
+            (((1,), (1,)), ((), ())),
+            preferred_element_type=F32,
+        ) * size ** (-0.5)
+        weight = jnp.exp(scores - jnp.max(scores, axis=1, keepdims=True))
+        weights.append(weight.astype(BF16))
+        totals.append(jnp.sum(weight, axis=1, keepdims=True))
     gather_forward(kv.at[1], 1, kv_states[1])
     z_end(out_state)
     gather_wait(kv_states[1])
@@ -539,31 +560,31 @@
     mixed = []
     for pair in range(width // 128):
         v = values[:, 128 * pair : 128 * pair + 128]
-        halves = []
-        for k in (2 * pair, 2 * pair + 1):
-            upper = weights[k].astype(BF16)
-            lower = (weights[k] - upper.astype(F32)).astype(BF16)
-            halves.append((dot(upper, v) + dot(lower, v)) / totals[k])
-        mixed.append(jnp.where(side, halves[0], halves[1]).astype(BF16))
+        attended = dot(weights[pair], v) / totals[pair]
+        mixed.append(jnp.where(side, attended[:own], attended[own:]).astype(BF16))
     mixed = jnp.concatenate(mixed, axis=1)
 
     gather_wait(out_state[2:])
+    per_head = w_out.shape[0] // heads
+
+    def out_term(k):
+        block = w_out[pl.ds(per_head * k, per_head)].reshape(width, width)
+        return lax.dot_general(
+            mixed, block, (((1,), (1,)), ((), ())), preferred_element_type=F32
+        )
+
     for k in range(heads):
-        per_head = w_out.shape[0] // heads
-        block = w_out[per_head * k : per_head * (k + 1)].reshape(width, width)
-        out_terms[k] = lax.dot_general(
-            mixed, block, (((1,), (1,)), ((), ())), preferred_element_type=F32
-        )
+        out_terms[k] = out_term(k).astype(BF16)
     end_copies = []
     for d in range(1, heads):
         to = lax.rem(h + d, heads)
         end_copies.append(
             remote(out_terms.at[to], out_in.at[d - 1], end_s.at[d], end_r.at[d], (r, to))
         )
-    result = out_terms[h]
+    result = out_term(h)
     for d, copy in enumerate(end_copies, 1):
         copy.wait_recv()
-        result = result + out_in[d - 1]
+        result = result + out_in[d - 1].astype(F32)
     out_ref[...] = result.astype(BF16)
     for copy in started:
         copy.wait_send()
@@ -595,10 +616,11 @@
                 pltpu.VMEM((2, own, width), F32),
                 pltpu.VMEM((own, width), F32),
                 pltpu.VMEM((rows, pad // 2, pixels), BF16),
-                pltpu.VMEM((rows, 2, pad, pixels), BF16),
-                pltpu.VMEM((per * 128, VARIANTS * width), BF16),
-                pltpu.VMEM((per * token_rows, rows * 2 * pad), BF16),
-                pltpu.VMEM((groups * token_rows, per * 128), BF16),
+                pltpu.VMEM((2, rows, 2, pad // 2, pixels), BF16),
+                pltpu.VMEM((pad * 128, VARIANTS * width), BF16),
+                pltpu.VMEM((2, pad // 2 * token_rows, rows * pad), BF16),
+                pltpu.VMEM((groups * token_rows, pad // 2 * 128), BF16),
+                pltpu.VMEM((groups * token_rows, VARIANTS * width), F32),
                 pltpu.VMEM((2, rows, groups * TROWS, 2 * width), BF16),
                 pltpu.VMEM((2, rows, groups * TROWS, 2 * width), BF16),
                 pltpu.VMEM((heads, tokens, width), BF16),
@@ -606,8 +628,8 @@
                 pltpu.VMEM((rows, wq.shape[0], width), BF16),
                 pltpu.VMEM((rows, wo.shape[0], width), BF16),
                 pltpu.VMEM((2, rows, tokens, width), BF16),
-                pltpu.VMEM((heads, own, width), F32),
-                pltpu.VMEM((heads - 1, own, width), F32),
+                pltpu.VMEM((heads, own, width), BF16),
+                pltpu.VMEM((heads - 1, own, width), BF16),
                 dma((9,)),
                 dma((4, rows)),
                 dma((4, rows)),

time: 57.4 us -> 56.7 us (0.988)
  Pallas kernels: 55.8 us -> 55.1 us
    pallas_call x1, Pallas kernels: 55.8 us -> 55.1 us  [per_chip(): pl.pallas_call(functools.partial(strip_kernel, rows, heads), out_shape=ja...]
where the time goes in v5:
time: 56.7 us; the launch traced here: 56.5 us
  Pallas kernels  55.1 us (97%)
  local copies, waits for them, and re-layouts  1.38 us (2%)
    pallas_call x1, Pallas kernels, per_chip(): pl.pallas_call(functools.partial(strip_kernel, rows, heads), out_shape=ja...  55.1 us
    unnamed x1, local copies, waits for them, and re-layouts  1.38 us

profile of v5, /device:TPU:0, one launch (start us, length us, event | category | flops | bytes accessed | tf_op | source)
XLA Modules:
  0.0 56.5 jit_solution(14175705242737813794)
XLA Ops:
  0.0 55.1 %shard_map.91 = bf16[64,256]{1,0:T(8,128)(2,1)} custom-call(bf16[5,64,1024]{2,1,0:T(8,128)(2,1)} %image_ref.1, bf16[1440,256]{1,0:T(8,128)(2,1)} %stem_ref.1, bf16[1024]{0:T(1024)(128)(2,1)} %token_gain_ref.1, bf16[512,1024]{1,0:T(8,128)(2,1)} %latents_ref.1, bf16[1024]{0:T(1024)(128)(2,1)} %latent_gain_ref.1, bf16[128,256]{1,0:T(8,128)(2,1)} %wq_ref.1, ...), custom_call_target="tpu_custom_call" | custom-call | tf_op jit(solution)/shard_map/pallas_call | solution.py:604
  55.2 1.4 %copy.11 = bf16[64,256]{1,0:T(8,128)(2,1)} copy(bf16[64,256]{1,0:T(8,128)(2,1)} %shard_map.91) | data formatting | bytes 65536

commit v6 on v5

--- a/solution.py
+++ b/solution.py
@@ -177,7 +177,8 @@
     part_out,
     part_in,
     feature,
-    w_first,
+    w_key,
+    w_value,
     w_query,
     w_out,
     kv,
@@ -226,8 +227,8 @@
         for k, (source, target) in enumerate(
             [
                 (image_ref, image),
-                (wk_ref, w_first.at[r, 0]),
-                (wv_ref, w_first.at[r, 1]),
+                (wk_ref, w_key.at[r]),
+                (wv_ref, w_value.at[r]),
                 (stem_ref, stem),
                 (wq_ref, w_query.at[r]),
                 (wo_ref, w_out.at[r]),
@@ -295,7 +296,7 @@
             for d in range(1, rows // 2)
         ]
         across = remote(
-            buf.at[r], buf.at[r], gy_s.at[3 + which, 0], gy_r.at[3 + which, 0], (y_peer, h)
+            buf.at[r], buf.at[r], gy_s.at[4 + which, 0], gy_r.at[4 + which, 0], (y_peer, h)
         )
         return first, [across]
 
@@ -308,8 +309,8 @@
                 remote(
                     buf.at[slot],
                     buf.at[slot],
-                    gy_s.at[3 + which, d],
-                    gy_r.at[3 + which, d],
+                    gy_s.at[4 + which, d],
+                    gy_r.at[4 + which, d],
                     (y_peer, h),
                 )
             )
@@ -319,10 +320,10 @@
             copy.wait_recv()
 
     def z_start(buf, which, over_y=True):
-        first = [
-            remote(buf.at[r], buf.at[r], z_s.at[which, 0], z_r.at[which, 0], (z_opposite, h)),
-            remote(buf.at[r], buf.at[r], z_s.at[which, 1], z_r.at[which, 1], (z_pair, h)),
-        ]
+        own_slot = buf.at[r]
+        pair = remote(
+            own_slot, own_slot, z_s.at[which, 1], z_r.at[which, 1], (z_pair, h)
+        )
         across = []
 
         def y_send(slot):
@@ -334,21 +335,32 @@
                 )
 
         y_send(r)
-        return buf, which, first, across, y_send
-
-    def z_pass(state):
-        buf, which, first, across, y_send = state
-        first[0].wait_recv()
-        ref = buf.at[z_opposite]
-        first.append(remote(ref, ref, z_s.at[which, 2], z_r.at[which, 2], (z_pair, h)))
-        y_send(z_opposite)
-        first[1].wait_recv()
-        y_send(z_pair)
+        return {"buf": buf, "which": which, "pair": pair, "across": across, "y": y_send}
+
+    def z_far(state):
+        ref, which = state["buf"].at[r], state["which"]
+        state["far"] = remote(
+            ref, ref, z_s.at[which, 0], z_r.at[which, 0], (z_opposite, h)
+        )
+
+    def z_near_pass(state):
+        state["pair"].wait_recv()
+        state["y"](z_pair)
+
+    def z_far_pass(state):
+        which = state["which"]
+        state["far"].wait_recv()
+        ref = state["buf"].at[z_opposite]
+        state["last"] = remote(ref, ref, z_s.at[which, 2], z_r.at[which, 2], (z_pair, h))
+        state["y"](z_opposite)
 
     def z_end(state):
-        buf, which, first, across, y_send = state
-        first[2].wait_recv()
-        y_send(z_last)
+        state["last"].wait_recv()
+        state["y"](z_last)
+
+    def all_in(state):
+        for copy in state["across"]:
+            copy.wait_recv()
 
     far_first = (4, 3, 5, 2, 6, 1, 7)
     line_copies = []
@@ -363,6 +375,9 @@
                 (to, h),
             )
         )
+    loads[1].wait()
+    loads[2].wait()
+    first_states = [z_start(w_key, 0), z_start(w_value, 3)]
     for part in range(2):
         row = iota((2 * quarter, 1), 0)
         lines_in[part, r] = pick(
@@ -409,9 +424,9 @@
         slot = lax.rem(r + rows - d, rows)
         over_x.append(pass_line(slot, half, 1, d, x_peer))
         over_core.append(pass_line(slot, half, 2, d, core_peer))
-    loads[1].wait()
-    loads[2].wait()
-    first_state = z_start(w_first, 0)
+    for state in first_states:
+        z_far(state)
+        z_near_pass(state)
     def order_lines(part):
         lines = dot(
             order[part], lines_in[part].reshape(rows * 2 * quarter, pixels)
@@ -441,7 +456,8 @@
     for copy in last_lines:
         copy.wait_recv()
     order_lines(1 - half)
-    z_pass(first_state)
+    for state in first_states:
+        z_far_pass(state)
 
     each = groups * TROWS
     row = iota((rows * each, 1), 0)
@@ -475,6 +491,7 @@
     send_sums(1, [both(2), both(3) + rim])
     loads[4].wait()
     query_state = z_start(w_query, 1, over_y=False)
+    z_far(query_state)
 
     def norm(x, gain_ref):
         average = jnp.mean(x, axis=-1, keepdims=True)
@@ -484,7 +501,8 @@
             BF16
         )
 
-    z_end(first_state)
+    for state in first_states:
+        z_end(state)
     for copy in loads[6:]:
         copy.wait()
     latent_norm[...] = norm(latent_rows[...].astype(F32), latent_gain)
@@ -508,16 +526,20 @@
         )
     loads[5].wait()
     out_state = z_start(w_out, 2)
-    z_pass(query_state)
-    gather_wait(first_state[2:])
+    z_far(out_state)
+    z_near_pass(query_state)
+    z_far_pass(query_state)
+    all_in(first_states[0])
     for copy in feat_copies:
         copy.wait_recv()
     token_norm = norm(
         jnp.concatenate([feature[k] for k in range(heads)], axis=1).astype(F32), token_gain
     )
     kv_states = []
-    for k in range(2):
-        kv[k, r] = dot(token_norm, w_first[:, k].reshape(D, width)).astype(BF16)
+    for k, weight in enumerate((w_key, w_value)):
+        if k == 1:
+            all_in(first_states[1])
+        kv[k, r] = dot(token_norm, weight[...].reshape(D, width)).astype(BF16)
         kv_states.append(gather_start(kv.at[k], k))
     z_end(query_state)
     depth = wq_ref.shape[0]
@@ -529,7 +551,8 @@
         )
     query_part[...] = part.reshape(query_part.shape)
     query_copy = remote(query_part.at[1 - y], query_in, query_s, query_r, (y_peer, h))
-    z_pass(out_state)
+    z_near_pass(out_state)
+    z_far_pass(out_state)
     gather_forward(kv.at[0], 0, kv_states[0])
     query_copy.wait_recv()
     queries = (query_part[y] + query_in[...]).astype(BF16)
@@ -564,7 +587,7 @@
         mixed.append(jnp.where(side, attended[:own], attended[own:]).astype(BF16))
     mixed = jnp.concatenate(mixed, axis=1)
 
-    gather_wait(out_state[2:])
+    all_in(out_state)
     per_head = w_out.shape[0] // heads
 
     def out_term(k):
@@ -624,7 +647,8 @@
                 pltpu.VMEM((2, rows, groups * TROWS, 2 * width), BF16),
                 pltpu.VMEM((2, rows, groups * TROWS, 2 * width), BF16),
                 pltpu.VMEM((heads, tokens, width), BF16),
-                pltpu.VMEM((rows, 2, wk.shape[0], width), BF16),
+                pltpu.VMEM((rows, wk.shape[0], width), BF16),
+                pltpu.VMEM((rows, wv.shape[0], width), BF16),
                 pltpu.VMEM((rows, wq.shape[0], width), BF16),
                 pltpu.VMEM((rows, wo.shape[0], width), BF16),
                 pltpu.VMEM((2, rows, tokens, width), BF16),
@@ -641,12 +665,12 @@
                 dma((heads,)),
                 dma((heads,)),
                 dma((heads,)),
-                dma((3, 3)),
-                dma((3, 3)),
+                dma((4, 3)),
+                dma((4, 3)),
                 dma((2, rows // 2)),
                 dma((2, rows // 2)),
-                dma((5, rows // 2)),
-                dma((5, rows // 2)),
+                dma((6, rows // 2)),
+                dma((6, rows // 2)),
             ],
             compiler_params=pltpu.CompilerParams(
                 collective_id=0, has_side_effects=True, vmem_limit_bytes=60 * 2**20

time: 56.7 us -> 56.3 us (level)
  no operation moved by 1% of the time
where the time goes in v6:
time: 56.3 us; the launch traced here: 56.1 us
  Pallas kernels  54.7 us (97%)
  local copies, waits for them, and re-layouts  1.38 us (2%)
    pallas_call x1, Pallas kernels, per_chip(): pl.pallas_call(functools.partial(strip_kernel, rows, heads), out_shape=ja...  54.7 us
    unnamed x1, local copies, waits for them, and re-layouts  1.38 us

profile of v6, /device:TPU:0, one launch (start us, length us, event | category | flops | bytes accessed | tf_op | source)
XLA Modules:
  0.0 56.1 jit_solution(13247569004342772625)
XLA Ops:
  0.0 54.7 %shard_map.91 = bf16[64,256]{1,0:T(8,128)(2,1)} custom-call(bf16[5,64,1024]{2,1,0:T(8,128)(2,1)} %image_ref.1, bf16[1440,256]{1,0:T(8,128)(2,1)} %stem_ref.1, bf16[1024]{0:T(1024)(128)(2,1)} %token_gain_ref.1, bf16[512,1024]{1,0:T(8,128)(2,1)} %latents_ref.1, bf16[1024]{0:T(1024)(128)(2,1)} %latent_gain_ref.1, bf16[128,256]{1,0:T(8,128)(2,1)} %wq_ref.1, ...), custom_call_target="tpu_custom_call" | custom-call | tf_op jit(solution)/shard_map/pallas_call | solution.py:627
  54.8 1.4 %copy.11 = bf16[64,256]{1,0:T(8,128)(2,1)} copy(bf16[64,256]{1,0:T(8,128)(2,1)} %shard_map.91) | data formatting | bytes 65536
